TPU v7x, 128 devices: a whole 4x4x4 slice. The times are simulated.
128 devices in a mesh: dp: 8 (over x, core), mem: 16 (over z, y).
Axes of the slice: x: 4, y: 4, z: 4, core: 2. Of those that a mesh axis runs over, the one named last changes fastest.
Arguments:
- tokens: bfloat16 [256, 256, 1024], P(('dp', 'mem')), may hold values from -6 to 6
- memory: bfloat16 [256, 384, 1024], P('dp', 'mem'), may hold values from -6 to 6
- cotangent: bfloat16 [256, 256, 1024], P(('dp', 'mem')), may hold values from -24 to 24
- tgt_len: int32 [256], P(('dp', 'mem')), may hold values from 128 to 256, as said below
- src_len: int32 [256], P('dp'), may hold values from 24 to 384, as said below
- self_qkv: bfloat16 [1024, 3072], P('dp'), may hold values from -0.1875 to 0.1875
- self_out: bfloat16 [1024, 1024], P('dp'), may hold values from -0.75 to 0.75
- cross_q: bfloat16 [1024, 1024], P('dp'), may hold values from -0.1875 to 0.1875
- cross_kv: bfloat16 [1024, 2048], P('dp'), may hold values from -0.1875 to 0.1875
- cross_out: bfloat16 [1024, 1024], P('dp'), may hold values from -1 to 1
- ffn_in: bfloat16 [1024, 4096], P('dp'), may hold values from -0.1875 to 0.1875
- ffn_out: bfloat16 [4096, 1024], P('dp'), may hold values from -0.09375 to 0.09375
- first_gain: bfloat16 [1024], P('dp'), may hold values from 0.5 to 1.5
- first_bias: bfloat16 [1024], P('dp'), may hold values from -1 to 1
- second_gain: bfloat16 [1024], P('dp'), may hold values from 0.5 to 1.5
- second_bias: bfloat16 [1024], P('dp'), may hold values from -1 to 1
- third_gain: bfloat16 [1024], P('dp'), may hold values from 0.5 to 1.5
- third_bias: bfloat16 [1024], P('dp'), may hold values from -1 to 1
- prefix_key: bfloat16 [30, 1024], replicated, may hold values from -6 to 6
- prefix_value: bfloat16 [30, 1024], replicated, may hold values from -6 to 6
- down_weight: bfloat16 [1024, 512], replicated, may hold values from -0.1875 to 0.1875
- down_bias: bfloat16 [512], replicated, may hold values from -3 to 3
- up_weight: bfloat16 [512, 1024], replicated, may hold values from -0.0625 to 0.0625
- up_bias: bfloat16 [1024], replicated, may hold values from -0.59765625 to 0.59765625
Outputs:
- output: bfloat16 [256, 256, 1024], P(('dp', 'mem'))
- input_grad: bfloat16 [256, 256, 1024], P(('dp', 'mem'))
- memory_grad: bfloat16 [256, 384, 1024], P('dp', 'mem')
- keyprefix_grad: float32 [30, 1024], P(None, ('dp', 'mem'))
- valueprefix_grad: float32 [30, 1024], P(None, ('dp', 'mem'))
- downweight_grad: float32 [1024, 512], P(('dp', 'mem'))
- downbias_grad: float32 [512], P(('dp', 'mem'))
- upweight_grad: float32 [512, 1024], P(None, ('dp', 'mem'))
- upbias_grad: float32 [1024], P(('dp', 'mem'))
Inputs may be any that keep to these rules, and one draw needn't show every extreme that they name: `tgt_len`: sequences n with equal n // 32 and equal (n) % 2 form a group; each group holds one sequence of length 256 and another of half of 256. `src_len`: in each group as for tgt_len one sequence has 384 source positions and another has 24; short ones are more common.
All inputs are finite; a program needn't handle non-finite values.
Results may differ from a plain program's by a relative error of at most 0.023.
Values may be sent and summed in bfloat16 or wider, within the bound.
No kernel may reach another device: no remote copies, remote signals or barrier semaphores. Data moves between devices by JAX's collectives and lax.ppermute only.
A program may use at most 256 MiB of HBM per device.

v0:
```python
import jax
import jax.numpy as jnp
from jax import lax
from jax.sharding import Mesh
from jax.sharding import PartitionSpec as P

HEAD_DIM = 64
MICRO = 2
MEM = ("mem_0", "mem_1")
DP = ("dp_0", "dp_1")
DP_MEM = ("dp_0", "dp_1", "mem_0", "mem_1")


NEGATIVE = -1e30
EPSILON = 1e-05


def side_by_side(arrays, axis, dim, along):
    both = jnp.concatenate(arrays, axis=along)
    filled, at, finished = (lax.all_gather(both, axis, axis=dim, tiled=True), 0, [])
    for a in arrays:
        finished.append(lax.slice_in_dim(filled, at, at + a.shape[along], axis=along))
        at += a.shape[along]
    return tuple(finished)


def in_blocks(x, dim, size):
    shape = x.shape
    tiles = x.reshape(*shape[:dim], size, shape[dim] // size, *shape[dim + 1 :])
    return jnp.moveaxis(tiles, dim, 0)


def sent_and_summed(x, axis, dim):
    tiles = in_blocks(x, dim, lax.axis_size(axis))
    arrived = lax.all_to_all(tiles, axis, split_axis=0, concat_axis=0, tiled=True)
    return arrived.sum(axis=0)


def sum_by_axis(x, axes, dim):
    far, near = axes
    tiles = in_blocks(x, dim, lax.axis_size(far))
    nearer = sent_and_summed(tiles, near, dim + 1)
    arrived = lax.all_to_all(nearer, far, split_axis=0, concat_axis=0, tiled=True)
    return arrived.sum(axis=0)


def sent_together(arrays, axis, dim, along):
    widths = [a.shape[along] for a in arrays]
    both = jnp.concatenate(arrays, axis=along)
    filled = sum_by_axis(both, axis, dim)
    return tuple(jnp.split(filled, [sum(widths[:k]) for k in range(1, len(widths))], axis=along))


def product(left, right):
    return jnp.dot(left, right, preferred_element_type=jnp.float32)


def back_product(grad_in, weight_in):
    return lax.dot_general(
        grad_in,
        weight_in,
        (((grad_in.ndim - 1,), (1,)), ((), ())),
        preferred_element_type=jnp.float32,
    )


def weight_grad(left, right):
    return lax.dot_general(
        left, right, (((0, 1), (0, 1)), ((), ())), preferred_element_type=jnp.float32
    )


def normalize(hidden, gain, offset):
    centred = hidden - jnp.mean(hidden, axis=-1, keepdims=True)
    inverse = lax.rsqrt(jnp.mean(centred * centred, axis=-1, keepdims=True) + EPSILON)
    normed = centred * inverse
    return (normed * gain + offset, normed, inverse)


def normalize_back(grad_in, normed, inverse, gain):
    scaled = grad_in * gain
    return inverse * (
        scaled
        - jnp.mean(scaled, axis=-1, keepdims=True)
        - normed * jnp.mean(scaled * normed, axis=-1, keepdims=True)
    )


def gelu_exact(value_in):
    return jax.nn.gelu(value_in, approximate=False)


def gelu_back(pre_act, grad_in):
    return jax.vjp(gelu_exact, pre_act)[1](grad_in)[0]


def split_heads(array_in):
    return array_in.reshape(array_in.shape[:-1] + (array_in.shape[-1] // HEAD_DIM, HEAD_DIM))


def cross_scores(query_in, key_in):
    return jnp.einsum(
        "gkhd,gqhd->ghkq",
        split_heads(key_in),
        split_heads(query_in),
        preferred_element_type=jnp.float32,
    ) * HEAD_DIM ** (-0.5)


def cross_weights(scores_in, valid_in, row_shift):
    return jnp.exp(
        jnp.where(valid_in[:, None, :, None], scores_in - row_shift[:, :, None, :], NEGATIVE)
    )


def cross_back(query_in, key_in, value_in, valid_in, row_shift, numer_grad, row_delta, w_ckv):
    weights_now = cross_weights(cross_scores(query_in, key_in), valid_in, row_shift)
    key_heads = split_heads(key_in)
    prob_grad = jnp.einsum(
        "gqhd,gkhd->ghkq", numer_grad, split_heads(value_in), preferred_element_type=jnp.float32
    )
    score_grad = (weights_now * (prob_grad - row_delta[:, :, None, :])).astype(jnp.bfloat16)
    factor = HEAD_DIM ** (-0.5)
    query_grad = (
        jnp.einsum("ghkq,gkhd->gqhd", score_grad, key_heads, preferred_element_type=jnp.float32)
        * factor
    )
    key_grad = (
        jnp.einsum(
            "ghkq,gqhd->gkhd", score_grad, split_heads(query_in), preferred_element_type=jnp.float32
        )
        * factor
    ).astype(jnp.bfloat16)
    value_grad = jnp.einsum(
        "ghkq,gqhd->gkhd",
        weights_now.astype(jnp.bfloat16),
        numer_grad,
        preferred_element_type=jnp.float32,
    ).astype(jnp.bfloat16)
    joined = jnp.concatenate(
        [key_grad.reshape(key_in.shape), value_grad.reshape(value_in.shape)], axis=-1
    )
    return (query_grad.reshape(query_in.shape), back_product(joined, w_ckv))


def local(
    tokens,
    memory,
    cotangent,
    tgt_len,
    src_len,
    self_qkv,
    self_out,
    cross_q,
    cross_kv,
    cross_out,
    ffn_in,
    ffn_out,
    first_gain,
    first_bias,
    second_gain,
    second_bias,
    third_gain,
    third_bias,
    prefix_key,
    prefix_value,
    down_weight,
    down_bias,
    up_weight,
    up_bias,
):
    mem_groups = lax.axis_size(MEM)
    mem_place = lax.axis_index(MEM)
    seq_local = tokens.shape[0] // MICRO
    tgt_size = tokens.shape[1]
    model_width = tokens.shape[2]
    src_block = memory.shape[1]
    prefix_size = prefix_key.shape[0]
    factor = HEAD_DIM ** (-0.5)
    frozen = (
        self_qkv,
        self_out,
        cross_q,
        cross_kv,
        cross_out,
        ffn_in,
        ffn_out,
        first_gain,
        first_bias,
        second_gain,
        second_bias,
        third_gain,
        third_bias,
    )
    memory_view = memory.reshape(mem_groups, MICRO, seq_local, src_block, model_width)
    source_view = src_len.reshape(mem_groups, MICRO, seq_local)
    positions = jnp.arange(tgt_size)
    causal_base = positions[None, :] <= positions[:, None]
    grad_sums = tuple(
        (
            jnp.zeros(shape_in, jnp.float32)
            for shape_in in (
                prefix_key.shape,
                prefix_value.shape,
                down_weight.shape,
                down_bias.shape,
                up_weight.shape,
                up_bias.shape,
            )
        )
    )
    output_parts, input_parts, memory_parts = ([], [], [])
    for micro_index in range(MICRO):
        weights_now = (
            *side_by_side(
                (frozen[0], frozen[1], frozen[2], frozen[3], frozen[4], frozen[5]), DP, 0, 1
            ),
            lax.all_gather(frozen[6], DP, axis=0, tiled=True),
            lax.all_gather(frozen[7], DP, axis=0, tiled=True),
            lax.all_gather(frozen[8], DP, axis=0, tiled=True),
            lax.all_gather(frozen[9], DP, axis=0, tiled=True),
            lax.all_gather(frozen[10], DP, axis=0, tiled=True),
            lax.all_gather(frozen[11], DP, axis=0, tiled=True),
            lax.all_gather(frozen[12], DP, axis=0, tiled=True),
        )
        w_qkv, w_out, w_cq, w_ckv, w_cout, w_in, w_ffout = weights_now[:7]
        gain_one, bias_one, gain_two, bias_two, gain_three, bias_three = [
            vector_in.astype(jnp.float32) for vector_in in weights_now[7:]
        ]
        lo_row = micro_index * seq_local
        tok_here = tokens[lo_row : lo_row + seq_local]
        len_here = tgt_len[lo_row : lo_row + seq_local]
        row_valid = positions[None, :] < len_here[:, None]
        visible = jnp.concatenate(
            [
                jnp.ones((seq_local, tgt_size, prefix_size), jnp.bool_),
                causal_base[None] & row_valid[:, None, :],
            ],
            axis=2,
        )[:, None]
        projected = product(tok_here, w_qkv)
        self_query = split_heads(projected[..., :model_width].astype(jnp.bfloat16))
        self_key = projected[..., model_width : 2 * model_width].astype(jnp.bfloat16)
        self_value = projected[..., 2 * model_width :].astype(jnp.bfloat16)
        key_all = split_heads(jnp.concatenate([prefix_key[None], self_key], axis=1))
        value_all = split_heads(jnp.concatenate([prefix_value[None], self_value], axis=1))

        def self_scores():
            scores_raw = (
                jnp.einsum(
                    "bqhd,bkhd->bhqk", self_query, key_all, preferred_element_type=jnp.float32
                )
                * factor
            )
            return jnp.where(visible, scores_raw, NEGATIVE)

        scores_now = self_scores()
        self_lse = jax.nn.logsumexp(scores_now, axis=-1, keepdims=True)
        attended = jnp.einsum(
            "bhqk,bkhd->bqhd",
            jax.nn.softmax(scores_now, axis=-1).astype(jnp.bfloat16),
            value_all,
            preferred_element_type=jnp.float32,
        )
        attended = attended.reshape(seq_local, tgt_size, model_width).astype(jnp.bfloat16)
        first_out, normed_one, inverse_one = normalize(
            tok_here.astype(jnp.float32) + product(attended, w_out), gain_one, bias_one
        )
        cross_query = product(first_out.astype(jnp.bfloat16), w_cq).astype(jnp.bfloat16)
        mem_here = memory_view[:, micro_index].reshape(
            mem_groups * seq_local, src_block, model_width
        )
        own_source = lax.dynamic_slice_in_dim(source_view[:, micro_index], mem_place, 1, 0).reshape(
            seq_local
        )
        mem_rows = lax.all_to_all(mem_here, MEM, split_axis=0, concat_axis=1, tiled=True)
        src_valid = jnp.arange(mem_rows.shape[1])[None, :] < own_source[:, None]
        kv_proj = product(mem_rows, w_ckv)
        mem_key = kv_proj[..., :model_width].astype(jnp.bfloat16)
        mem_value = kv_proj[..., model_width:].astype(jnp.bfloat16)
        scores_cross = cross_scores(cross_query, mem_key)
        local_max = jnp.max(jnp.where(src_valid[:, None, :, None], scores_cross, NEGATIVE), axis=2)
        weights_cross = cross_weights(scores_cross, src_valid, local_max)
        numer_part = jnp.einsum(
            "ghkq,gkhd->gqhd",
            weights_cross.astype(jnp.bfloat16),
            split_heads(mem_value),
            preferred_element_type=jnp.float32,
        )
        total_part = jnp.sum(weights_cross, axis=2)
        numerator, row_total = (numer_part, total_part)
        total_rows = jnp.transpose(row_total, (0, 2, 1))[..., None]
        merged = numerator / total_rows
        merged_low = merged.reshape(seq_local, tgt_size, model_width).astype(jnp.bfloat16)
        second_out, normed_two, inverse_two = normalize(
            first_out + product(merged_low, w_cout), gain_two, bias_two
        )
        second_low = second_out.astype(jnp.bfloat16)
        ffn_pre = product(second_low, w_in)
        ffn_act = gelu_exact(ffn_pre).astype(jnp.bfloat16)
        adapt_pre = product(second_low, down_weight) + down_bias.astype(jnp.float32)
        adapt_act = gelu_exact(adapt_pre).astype(jnp.bfloat16)
        hidden_three = (
            second_out
            + product(ffn_act, w_ffout)
            + 4.0 * (product(adapt_act, up_weight) + up_bias.astype(jnp.float32))
        )
        result, normed_three, inverse_three = normalize(hidden_three, gain_three, bias_three)
        output_parts.append(result.astype(jnp.bfloat16))
        grad_out = cotangent[lo_row : lo_row + seq_local].astype(jnp.float32) * row_valid[
            ..., None
        ].astype(jnp.float32)
        grad_three = normalize_back(grad_out, normed_three, inverse_three, gain_three)
        ffn_grad = grad_three.astype(jnp.bfloat16)
        adapt_grad = (4.0 * grad_three).astype(jnp.bfloat16)
        ffn_pre_grad = gelu_back(ffn_pre, back_product(ffn_grad, w_ffout)).astype(jnp.bfloat16)
        adapt_pre_grad = gelu_back(adapt_pre, back_product(adapt_grad, up_weight)).astype(
            jnp.bfloat16
        )
        grad_second = (
            grad_three
            + back_product(ffn_pre_grad, w_in)
            + back_product(adapt_pre_grad, down_weight)
        )
        grad_two = normalize_back(grad_second, normed_two, inverse_two, gain_two)
        merged_grad = split_heads(
            back_product(grad_two.astype(jnp.bfloat16), w_cout).astype(jnp.bfloat16)
        )
        numer_grad = (merged_grad.astype(jnp.float32) / total_rows).astype(jnp.bfloat16)
        row_delta = (
            jnp.transpose(jnp.sum(merged_grad.astype(jnp.float32) * merged, axis=-1), (0, 2, 1))
            / row_total
        )
        query_grad, memory_part = cross_back(
            cross_query, mem_key, mem_value, src_valid, local_max, numer_grad, row_delta, w_ckv
        )
        memory_parts.append(
            lax.all_to_all(
                memory_part.astype(jnp.bfloat16), MEM, split_axis=1, concat_axis=0, tiled=True
            )
        )
        grad_first = grad_two + back_product(query_grad.astype(jnp.bfloat16), w_cq)
        grad_one = normalize_back(grad_first, normed_one, inverse_one, gain_one)
        attended_grad = split_heads(
            back_product(grad_one.astype(jnp.bfloat16), w_out).astype(jnp.bfloat16)
        )
        probs_again = jnp.exp(self_scores() - self_lse)
        prob_grad = jnp.einsum(
            "bqhd,bkhd->bhqk", attended_grad, value_all, preferred_element_type=jnp.float32
        )
        score_grad = (
            probs_again * (prob_grad - jnp.sum(probs_again * prob_grad, axis=-1, keepdims=True))
        ).astype(jnp.bfloat16)
        key_grad = (
            jnp.einsum(
                "bhqk,bqhd->bkhd", score_grad, self_query, preferred_element_type=jnp.float32
            )
            * factor
        )
        query_grad_self = (
            jnp.einsum("bhqk,bkhd->bqhd", score_grad, key_all, preferred_element_type=jnp.float32)
            * factor
        )
        value_grad = jnp.einsum(
            "bhqk,bqhd->bkhd",
            probs_again.astype(jnp.bfloat16),
            attended_grad,
            preferred_element_type=jnp.float32,
        )
        row_shape = (seq_local, tgt_size, model_width)
        qkv_grad = jnp.concatenate(
            [
                query_grad_self.reshape(row_shape),
                key_grad[:, prefix_size:].reshape(row_shape),
                value_grad[:, prefix_size:].reshape(row_shape),
            ],
            axis=-1,
        ).astype(jnp.bfloat16)
        input_parts.append((grad_one + back_product(qkv_grad, w_qkv)).astype(jnp.bfloat16))
        grad_sums = (
            grad_sums[0]
            + jnp.sum(key_grad[:, :prefix_size], axis=0).reshape(prefix_size, model_width),
            grad_sums[1]
            + jnp.sum(value_grad[:, :prefix_size], axis=0).reshape(prefix_size, model_width),
            grad_sums[2] + weight_grad(second_low, adapt_pre_grad),
            grad_sums[3] + jnp.sum(adapt_pre_grad.astype(jnp.float32), axis=(0, 1)),
            grad_sums[4] + weight_grad(adapt_act, adapt_grad),
            grad_sums[5] + jnp.sum(adapt_grad.astype(jnp.float32), axis=(0, 1)),
        )
    output = jnp.concatenate(output_parts, axis=0)
    input_grad = jnp.concatenate(input_parts, axis=0)
    memory_all = jnp.stack(
        [
            part_in.reshape(mem_groups, seq_local, src_block, model_width)
            for part_in in memory_parts
        ],
        axis=1,
    ).reshape(memory.shape)
    summed = (
        *sent_together((grad_sums[0], grad_sums[1]), (("dp_0", "dp_1", "mem_0"), "mem_1"), 1, 0),
        sum_by_axis(grad_sums[2], (("dp_0", "dp_1", "mem_0"), "mem_1"), 0),
        sum_by_axis(grad_sums[3], (("dp_0", "dp_1", "mem_0"), "mem_1"), 0),
        sum_by_axis(grad_sums[4], (("dp_0", "dp_1", "mem_0"), "mem_1"), 1),
        sum_by_axis(grad_sums[5], (("dp_0", "dp_1", "mem_0"), "mem_1"), 0),
    )
    return (
        output,
        input_grad,
        memory_all,
        summed[0],
        summed[1],
        summed[2],
        summed[3],
        summed[4],
        summed[5],
    )


def solution(mesh):
    torus = Mesh(mesh.devices.reshape(4, 2, 4, 4), ("dp_0", "dp_1", "mem_0", "mem_1"))
    placed = (
        P(DP_MEM, None, None),
        P(DP, MEM, None),
        P(DP_MEM, None, None),
        P(DP_MEM),
        P(DP),
        P(DP, None),
        P(DP, None),
        P(DP, None),
        P(DP, None),
        P(DP, None),
        P(DP, None),
        P(DP, None),
        P(DP),
        P(DP),
        P(DP),
        P(DP),
        P(DP),
        P(DP),
        P(),
        P(),
        P(),
        P(),
        P(),
        P(),
    )
    return jax.shard_map(
        local,
        mesh=torus,
        in_specs=placed,
        out_specs=(
            P(DP_MEM, None, None),
            P(DP_MEM, None, None),
            P(DP, MEM, None),
            P(None, DP_MEM),
            P(None, DP_MEM),
            P(DP_MEM, None),
            P(DP_MEM),
            P(None, DP_MEM),
            P(DP_MEM),
        ),
        check_vma=False,
    )
```

profile of v0, /device:TPU:1, one launch (start us, length us, event | category | flops | bytes accessed | tf_op | source)
XLA Modules:
  0.0 628.3 jit_solution(9741097615081629005)
XLA Ops:
  19.0 8.6 %all-to-all-start.1 = ((bf16[16,24,1024]{2,1,0:T(8,128)(2,1)}), bf16[16,24,1024]{2,1,0:T(8,128)(2,1)}, u32[]{:S(2)}, u32[]{:S(2)}) async-start(bf16[16,24,1024]{2,1,0:T(8,128)(2,1)} %get-tuple-element.41), calls=%async_computation.1 | async-start | bytes 1572864 | tf_op jit(solution)/shard_map/all_to_all | solution.py:276
  32.3 11.2 %all-gather = bf16[8,1,128]{2,1,0:T(2,128)(2,1)S(1)} all-gather(bf16[1,1,128]{2,1,0:T(2,128)(2,1)S(1)} %bitcast.582), channel_id=1, replica_groups=mesh['dp_0'=4,'dp_1'=2,'mem_0'=4,'mem_1'=4] {'dp_0','dp_1'}, dimensions={0}, use_global_device_ids=true | all-gather | bytes 2304 | tf_op jit(solution)/shard_map/all_gather | solution.py:219
  43.5 8.1 %all-gather.1 = bf16[8,1,128]{2,1,0:T(2,128)(2,1)S(1)} all-gather(bf16[1,1,128]{2,1,0:T(2,128)(2,1)S(1)} %bitcast.583), channel_id=1, replica_groups=mesh['dp_0'=4,'dp_1'=2,'mem_0'=4,'mem_1'=4] {'dp_0','dp_1'}, dimensions={0}, use_global_device_ids=true | all-gather | bytes 2304 | tf_op jit(solution)/shard_map/all_gather | solution.py:220
  51.6 9.4 %all-gather.2 = bf16[8,1,128]{2,1,0:T(2,128)(2,1)S(1)} all-gather(bf16[1,1,128]{2,1,0:T(2,128)(2,1)S(1)} %bitcast.584), channel_id=1, replica_groups=mesh['dp_0'=4,'dp_1'=2,'mem_0'=4,'mem_1'=4] {'dp_0','dp_1'}, dimensions={0}, use_global_device_ids=true | all-gather | bytes 2304 | tf_op jit(solution)/shard_map/all_gather | solution.py:221
  61.0 8.0 %all-gather.3 = bf16[8,1,128]{2,1,0:T(2,128)(2,1)S(1)} all-gather(bf16[1,1,128]{2,1,0:T(2,128)(2,1)S(1)} %bitcast.585), channel_id=1, replica_groups=mesh['dp_0'=4,'dp_1'=2,'mem_0'=4,'mem_1'=4] {'dp_0','dp_1'}, dimensions={0}, use_global_device_ids=true | all-gather | bytes 2304 | tf_op jit(solution)/shard_map/all_gather | solution.py:222
  69.1 9.4 %all-gather.4 = bf16[8,1,128]{2,1,0:T(2,128)(2,1)S(1)} all-gather(bf16[1,1,128]{2,1,0:T(2,128)(2,1)S(1)} %bitcast.586), channel_id=1, replica_groups=mesh['dp_0'=4,'dp_1'=2,'mem_0'=4,'mem_1'=4] {'dp_0','dp_1'}, dimensions={0}, use_global_device_ids=true | all-gather | bytes 2304 | tf_op jit(solution)/shard_map/all_gather | solution.py:223
  79.1 8.0 %all-gather.5 = bf16[8,1,128]{2,1,0:T(2,128)(2,1)S(1)} all-gather(bf16[1,1,128]{2,1,0:T(2,128)(2,1)S(1)} %bitcast.587), channel_id=1, replica_groups=mesh['dp_0'=4,'dp_1'=2,'mem_0'=4,'mem_1'=4] {'dp_0','dp_1'}, dimensions={0}, use_global_device_ids=true | all-gather | bytes 2304 | tf_op jit(solution)/shard_map/all_gather | solution.py:224
  90.5 51.3 %all-gather.9.cloned.1.call-done = bf16[1024,12288]{1,0:T(8,128)(2,1)} async-done(((bf16[128,12288]{1,0:T(8,128)(2,1)}), bf16[1024,12288]{1,0:T(8,128)(2,1)}) %all-gather.9.cloned.1.call-update) | async-done | bytes 25165840 | tf_op jit(solution)/shard_map/all_gather | solution.py:20
  141.8 4.9 fusion.46
  169.8 6.6 %all-to-all-start = ((bf16[16,24,1024]{2,1,0:T(8,128)(2,1)}), bf16[16,24,1024]{2,1,0:T(8,128)(2,1)}, u32[]{:S(2)}, u32[]{:S(2)}) async-start(bf16[16,24,1024]{2,1,0:T(8,128)(2,1)} %get-tuple-element.40), calls=%async_computation | async-start | bytes 1572864 | tf_op jit(solution)/shard_map/all_to_all | solution.py:276
  176.4 4.8 fusion.69
  182.6 7.7 %fusion.429 = (f32[16,256]{1,0:T(8,128)S(1)}, f32[16,384,256]{2,1,0:T(8,128)}) fusion(pred[384]{0:T(512)(128)(4,1)S(1)} %iota_compare_fusion.1, bf16[384,16,64]{0,2,1:T(8,128)(2,1)} %bitcast.499, bf16[256,16,64]{0,2,1:T(8,128)(2,1)} %bitcast.515), kind=kOutput, calls=%fused_computation.481 | convolution fusion | flops 412090752 | bytes 7618944 | tf_op jit(solution)/shard_map/sub | solution.py:112
  190.3 4.9 fusion.430
  195.2 3.2 fusion.248
  204.3 4.8 fusion.66
  210.1 8.0 %fusion.424 = (f32[16,256]{1,0:T(8,128)S(1)}, f32[16,384,256]{2,1,0:T(8,128)}) fusion(pred[384]{0:T(512)(128)(4,1)S(1)} %iota_compare_fusion.2, bf16[384,16,64]{0,2,1:T(8,128)(2,1)} %bitcast.501, bf16[256,16,64]{0,2,1:T(8,128)(2,1)} %bitcast.517), kind=kOutput, calls=%fused_computation.476 | convolution fusion | flops 412090752 | bytes 7618944 | tf_op jit(solution)/shard_map/sub | solution.py:112
  218.8 4.4 fusion.425
  231.6 8.0 %fusion.16 = f32[256,4096]{1,0:T(8,128)} fusion(bf16[256,1024]{1,0:T(8,128)(2,1)S(1)} %get-tuple-element.52, bf16[1024,12288]{1,0:T(8,128)(2,1)} %all-gather.9.cloned.1.call-done), kind=kOutput, calls=%fused_computation.20 | convolution fusion | flops 2147483648 | bytes 13107200 | tf_op jit(solution)/shard_map/dot_general | solution.py:55
  239.5 14.3 %fusion.228 = f32[1,256,1024]{2,1,0:T(8,128)S(1)} fusion(bf16[4096,1024]{1,0:T(8,128)(2,1)} %all-gather.11.cloned.1.call-done, f32[256,4096]{1,0:T(8,128)} %fusion.16, f32[1,256,1024]{2,1,0:T(8,128)S(1)} %copy-done.18, f32[1024]{0:T(1024)S(1)} %bitcast.578, f32[1024]{0:T(1024)S(1)} %bitcast.573, f32[256]{0:T(256)S(1)} %add_rsqrt_fusion.4, ...), kind=kOutput, calls=%fused_computation.214 | convolution fusion | flops 2216951808 | bytes 14690304 | tf_op jit(solution)/shard_map/dot_general | solution.py:55
  254.9 6.1 fusion.14
  261.1 11.1 %fusion.229 = f32[1,256,1024]{2,1,0:T(8,128)S(1)} fusion(bf16[4096,1024]{1,0:T(8,128)(2,1)S(1)} %bitcast.589, f32[256,4096]{1,0:T(8,128)S(1)} %fusion.14, f32[1,256,1024]{2,1,0:T(8,128)S(1)} %copy-done.15, f32[256]{0:T(256)S(1)} %add_rsqrt_fusion.1, f32[256]{0:T(256)S(1)} %broadcast_multiply_fusion.13, f32[1024]{0:T(1024)S(1)} %bitcast.579, ...), kind=kOutput, calls=%fused_computation.215 | convolution fusion | flops 2216951808 | bytes 14690304 | tf_op jit(solution)/shard_map/dot_general | solution.py:55
  279.4 20.5 %fusion.410 = (f32[256]{0:T(256)S(1)}, f32[256]{0:T(256)S(1)}, f32[1,256,1024]{2,1,0:T(8,128)}) fusion(f32[256]{0:T(256)S(1)} %add_rsqrt_fusion.4, f32[1,256,1024]{2,1,0:T(8,128)S(1)} %copy-done.18, f32[256]{0:T(256)S(1)} %broadcast_multiply_fusion.16, f32[1024]{0:T(1024)S(1)} %bitcast.575, f32[1,256,1024]{2,1,0:T(8,128)} %convolution_bitcast_fusion.7, ...), kind=kOutput, calls=%fused_computation.464 | convolution fusion | flops 4372824064 | bytes 26222592 | tf_op jit(solution)/shard_map/dot_general | solution.py:59
  299.9 4.2 fusion.263
  308.6 5.2 fusion.118
  320.2 4.1 all-to-all-start.8
  324.3 3.2 fusion.409
  328.5 3.4 fusion.242
  334.4 23.2 %fusion.412 = (f32[256]{0:T(256)S(1)}, f32[256]{0:T(256)S(1)}, f32[1,256,1024]{2,1,0:T(8,128)}) fusion(f32[256]{0:T(256)S(1)} %add_rsqrt_fusion.1, f32[1,256,1024]{2,1,0:T(8,128)S(1)} %copy-done.16, f32[256]{0:T(256)S(1)} %broadcast_multiply_fusion.13, f32[1024]{0:T(1024)S(1)} %bitcast.576, f32[1,256,1024]{2,1,0:T(8,128)S(1)} %convolution_bitcast_fusion.6, ...), kind=kOutput, calls=%fused_computation.466 | convolution fusion | flops 4372824064 | bytes 26222592 | tf_op jit(solution)/shard_map/dot_general | solution.py:59
  357.6 3.8 fusion.260
  364.7 4.1 multiply_convert_fusion
  371.6 2.9 fusion.411
  375.5 3.4 fusion.245
  380.2 3.4 fusion.112
  383.7 4.3 multiply_reduce_fusion.1
  397.7 4.2 all-to-all-start.12
  406.6 4.2 all-to-all-start.4
  410.9 5.4 fusion.237
  419.0 8.8 %all-to-all-start.9 = ((f32[32,1,4]{2,1,0:T(1,128)}), f32[32,1,4]{2,1,0:T(1,128)S(1)}, u32[]{:S(2)}, u32[]{:S(2)}) async-start(f32[32,1,4]{2,1,0:T(1,128)} %bitcast.206), calls=%async_computation.9 | async-start | bytes 32768 | tf_op jit(solution)/shard_map/all_to_all | solution.py:43
  428.5 2.9 reduce.58
  435.2 6.7 %all-to-all-start.13 = ((f32[32,1,8]{2,1,0:T(1,128)}), f32[32,1,8]{2,1,0:T(1,128)}, u32[]{:S(2)}, u32[]{:S(2)}) async-start(f32[32,1,8]{2,1,0:T(1,128)} %copy.186), calls=%async_computation.13 | async-start | bytes 32768 | tf_op jit(solution)/shard_map/all_to_all | solution.py:43
  443.9 4.8 all-to-all-done.13
  448.7 4.6 all-to-all-start.5
  453.3 5.1 fusion.121
  461.3 7.3 %reduce.57 = bf16[384,1024]{1,0:T(8,128)(2,1)} reduce(bf16[384,1,1024]{2,1,0:T(2,128)(2,1)} %bitcast.489, bf16[]{:T(256)} %broadcast.1698), dimensions={1}, to_apply=%bitcast.469.reduce_sub_computation | reduce | bytes 1572866
  468.6 3.2 reshape.1534
  471.9 7.5 %all-to-all-start.2 = ((bf16[16,2,12288]{2,1,0:T(2,128)(2,1)}), bf16[16,2,12288]{2,1,0:T(2,128)(2,1)}, u32[]{:S(2)}, u32[]{:S(2)}) async-start(bf16[16,2,12288]{2,1,0:T(2,128)(2,1)} %reshape.1534), calls=%async_computation.2 | async-start | bytes 1572864 | tf_op jit(solution)/shard_map/all_to_all | solution.py:338
  479.4 3.2 multiply_convert_fusion.8
  482.6 4.0 fusion.234
  489.0 7.3 %reduce.56 = bf16[384,1024]{1,0:T(8,128)(2,1)} reduce(bf16[384,1,1024]{2,1,0:T(2,128)(2,1)} %bitcast.490, bf16[]{:T(256)} %broadcast.1698), dimensions={1}, to_apply=%bitcast.468.reduce_sub_computation | reduce | bytes 1572866
  496.3 3.2 reshape.1532
  499.5 6.8 %all-to-all-start.3 = ((bf16[16,2,12288]{2,1,0:T(2,128)(2,1)}), bf16[16,2,12288]{2,1,0:T(2,128)(2,1)}, u32[]{:S(2)}, u32[]{:S(2)}) async-start(bf16[16,2,12288]{2,1,0:T(2,128)(2,1)} %reshape.1532), calls=%async_computation.3 | async-start | bytes 1572864 | tf_op jit(solution)/shard_map/all_to_all | solution.py:338
  508.1 3.1 convolution_add_fusion
  511.2 3.0 copy.182
  514.2 3.1 copy.183
  519.3 4.7 all-to-all-start.10
  528.7 19.3 %all-to-all-done.10 = f32[4,32,512,8]{2,3,1,0:T(8,128)} async-done(((f32[4,32,512,8]{2,3,1,0:T(8,128)}), f32[4,32,512,8]{2,3,1,0:T(8,128)}, u32[]{:S(2)}, u32[]{:S(2)}) %all-to-all-start.10) | async-done | bytes 2097184 | tf_op jit(solution)/shard_map/all_to_all | solution.py:35
  548.0 4.4 all-to-all-start.6
  564.3 5.8 fusion.266
  572.7 2.8 all-to-all-done.6
  575.5 10.4 %all-to-all-start.11 = ((f32[32,512,8]{1,2,0:T(8,128)}), f32[32,512,8]{1,2,0:T(8,128)S(1)}, u32[]{:S(2)}, u32[]{:S(2)}) async-start(f32[32,512,8]{1,2,0:T(8,128)} %reduce_sum.502), calls=%async_computation.11 | async-start | bytes 1048576 | tf_op jit(solution)/shard_map/all_to_all | solution.py:43
  586.0 6.1 fusion.271
  596.9 5.3 all-to-all-start.7
  607.9 4.4 reshape.1535
  612.6 4.4 reshape.1533
  (479 shorter events, 156.7 us)
Async XLA Ops:
  7.2 219.3 %copy-start = (bf16[1024,512]{1,0:T(8,128)(2,1)S(1)}, bf16[1024,512]{1,0:T(8,128)(2,1)}, u32[]{:S(2)}) copy-start(bf16[1024,512]{1,0:T(8,128)(2,1)} %param.44) | copy-start | bytes 3145732
  7.2 134.6 %all-gather.9.cloned.1.call-start = ((), (), s32[]{:S(2)}) async-start(), calls=%async_computation.14 | async-start | bytes 28311552 | tf_op jit(solution)/shard_map/all_gather | solution.py:20
  7.2 9.3 %copy-start.61 = (bf16[128,4096]{1,0:T(8,128)(2,1)S(1)}, bf16[128,4096]{1,0:T(8,128)(2,1)}, u32[]{:S(2)}) copy-start(bf16[128,4096]{1,0:T(8,128)(2,1)} %param.34) | copy-start | bytes 3145732
  17.6 10.8 %copy-start.105 = (s32[2]{0:T(128)S(1)}, s32[2]{0:T(128)}, u32[]{:S(2)}) copy-start(s32[2]{0:T(128)} %param.27) | copy-start | bytes 28
  17.6 14.6 %copy-start.106 = (bf16[512]{0:T(512)(128)(2,1)S(1)}, bf16[512]{0:T(512)(128)(2,1)}, u32[]{:S(2)}) copy-start(bf16[512]{0:T(512)(128)(2,1)} %param.45) | copy-start | bytes 3076
  17.6 14.6 %copy-start.104 = (bf16[1024]{0:T(1024)(128)(2,1)S(1)}, bf16[1024]{0:T(1024)(128)(2,1)}, u32[]{:S(2)}) copy-start(bf16[1024]{0:T(1024)(128)(2,1)} %param.47) | copy-start | bytes 6148
  17.6 14.6 %copy-start.117 = (bf16[128]{0:T(256)(128)(2,1)S(1)}, bf16[128]{0:T(256)(128)(2,1)}, u32[]{:S(2)}) copy-start(bf16[128]{0:T(256)(128)(2,1)} %param.36) | copy-start | bytes 772
  17.6 25.9 %copy-start.118 = (bf16[128]{0:T(256)(128)(2,1)S(1)}, bf16[128]{0:T(256)(128)(2,1)}, u32[]{:S(2)}) copy-start(bf16[128]{0:T(256)(128)(2,1)} %param.37) | copy-start | bytes 772
  17.6 33.9 %copy-start.119 = (bf16[128]{0:T(256)(128)(2,1)S(1)}, bf16[128]{0:T(256)(128)(2,1)}, u32[]{:S(2)}) copy-start(bf16[128]{0:T(256)(128)(2,1)} %param.38) | copy-start | bytes 772
  17.6 43.4 %copy-start.120 = (bf16[128]{0:T(256)(128)(2,1)S(1)}, bf16[128]{0:T(256)(128)(2,1)}, u32[]{:S(2)}) copy-start(bf16[128]{0:T(256)(128)(2,1)} %param.39) | copy-start | bytes 772
  17.7 51.4 %copy-start.121 = (bf16[128]{0:T(256)(128)(2,1)S(1)}, bf16[128]{0:T(256)(128)(2,1)}, u32[]{:S(2)}) copy-start(bf16[128]{0:T(256)(128)(2,1)} %param.40) | copy-start | bytes 772
  17.7 61.5 %copy-start.122 = (bf16[128]{0:T(256)(128)(2,1)S(1)}, bf16[128]{0:T(256)(128)(2,1)}, u32[]{:S(2)}) copy-start(bf16[128]{0:T(256)(128)(2,1)} %param.41) | copy-start | bytes 772
  17.7 70.1 %copy-start.123 = (s32[32]{0:T(128)S(1)}, s32[32]{0:T(128)}, u32[]{:S(2)}) copy-start(s32[32]{0:T(128)} %param.28) | copy-start | bytes 388
  17.7 72.4 %copy-start.80 = (bf16[30,1024]{1,0:T(8,128)(2,1)S(1)}, bf16[30,1024]{1,0:T(8,128)(2,1)}, u32[]{:S(2)}) copy-start(bf16[30,1024]{1,0:T(8,128)(2,1)} %param.43) | copy-start | bytes 184324
  17.7 72.6 %copy-start.81 = (bf16[30,1024]{1,0:T(8,128)(2,1)S(1)}, bf16[30,1024]{1,0:T(8,128)(2,1)}, u32[]{:S(2)}) copy-start(bf16[30,1024]{1,0:T(8,128)(2,1)} %param.42) | copy-start | bytes 184324
  19.0 150.7 %all-to-all-start.1 = ((bf16[16,24,1024]{2,1,0:T(8,128)(2,1)}), bf16[16,24,1024]{2,1,0:T(8,128)(2,1)}, u32[]{:S(2)}, u32[]{:S(2)}) async-start(bf16[16,24,1024]{2,1,0:T(8,128)(2,1)} %get-tuple-element.41), calls=%async_computation.1 | async-start | bytes 1572864 | tf_op jit(solution)/shard_map/all_to_all | solution.py:276
  27.7 211.8 %all-gather.11.cloned.1.call-start = ((), (), s32[]{:S(2)}) async-start(), calls=%async_computation.15 | async-start | bytes 9437184 | tf_op jit(solution)/shard_map/all_gather | solution.py:218
  43.5 179.7 %copy-start.76 = (f32[8,1,128]{2,1,0:T(1,128)}, f32[8,1,128]{2,1,0:T(1,128)S(1)}, u32[]{:S(2)}) copy-start(f32[8,1,128]{2,1,0:T(1,128)S(1)} %convert_element_type.532) | copy-start | bytes 12292
  90.3 73.4 %copy-start.36 = (bf16[30,1024]{0,1:T(8,128)(2,1)}, bf16[30,1024]{0,1:T(8,128)(2,1)S(1)}, u32[]{:S(2)}) copy-start(bf16[30,1024]{0,1:T(8,128)(2,1)S(1)} %copy.161) | copy-start | bytes 184324
  90.5 69.4 %copy-start.34 = (bf16[30,1024]{0,1:T(8,128)(2,1)}, bf16[30,1024]{0,1:T(8,128)(2,1)S(1)}, u32[]{:S(2)}) copy-start(bf16[30,1024]{0,1:T(8,128)(2,1)S(1)} %copy.162) | copy-start | bytes 184324
  141.8 10.6 %slice-start.6 = ((s8[25165824]{0:T(1024)(128)(4,1)}), s8[4194304]{0:T(1024)(128)(4,1)S(1)}, s32[]{:S(2)}) async-start(s8[25165824]{0:T(1024)(128)(4,1)} %bitcast.503), calls=%async_computation.22 | async-start | bytes 8388608
  141.8 10.6 %slice-start.7 = ((s8[25165824]{0:T(1024)(128)(4,1)}), s8[4194304]{0:T(1024)(128)(4,1)S(1)}, s32[]{:S(2)}) async-start(s8[25165824]{0:T(1024)(128)(4,1)} %bitcast.503), calls=%async_computation.23 | async-start | bytes 8388608
  157.5 43.0 %copy-start.8 = (f32[1,256,1024]{2,1,0:T(8,128)}, f32[1,256,1024]{2,1,0:T(8,128)S(1)}, u32[]{:S(2)}) copy-start(f32[1,256,1024]{2,1,0:T(8,128)S(1)} %get-tuple-element.73) | copy-start | bytes 3145732
  157.5 42.9 %copy-start.85 = (f32[256]{0:T(256)}, f32[256]{0:T(256)S(1)}, u32[]{:S(2)}) copy-start(f32[256]{0:T(256)S(1)} %broadcast_multiply_fusion.14) | copy-start | bytes 3076
  157.8 42.7 %copy-start.91 = (f32[256]{0:T(256)}, f32[256]{0:T(256)S(1)}, u32[]{:S(2)}) copy-start(f32[256]{0:T(256)S(1)} %add_rsqrt_fusion.2) | copy-start | bytes 3076
  165.8 57.4 %copy-start.11 = (f32[1,256,1024]{2,1,0:T(8,128)}, f32[1,256,1024]{2,1,0:T(8,128)S(1)}, u32[]{:S(2)}) copy-start(f32[1,256,1024]{2,1,0:T(8,128)S(1)} %get-tuple-element.63) | copy-start | bytes 3145732
  169.5 53.8 %copy-start.88 = (f32[256]{0:T(256)}, f32[256]{0:T(256)S(1)}, u32[]{:S(2)}) copy-start(f32[256]{0:T(256)S(1)} %broadcast_multiply_fusion.17) | copy-start | bytes 3076
  169.7 53.5 %copy-start.94 = (f32[256]{0:T(256)}, f32[256]{0:T(256)S(1)}, u32[]{:S(2)}) copy-start(f32[256]{0:T(256)S(1)} %add_rsqrt_fusion.5) | copy-start | bytes 3076
  169.8 34.5 %all-to-all-start = ((bf16[16,24,1024]{2,1,0:T(8,128)(2,1)}), bf16[16,24,1024]{2,1,0:T(8,128)(2,1)}, u32[]{:S(2)}, u32[]{:S(2)}) async-start(bf16[16,24,1024]{2,1,0:T(8,128)(2,1)} %get-tuple-element.40), calls=%async_computation | async-start | bytes 1572864 | tf_op jit(solution)/shard_map/all_to_all | solution.py:276
  203.1 131.3 %copy-start.100 = (f32[256]{0:T(256)}, f32[256]{0:T(256)S(1)}, u32[]{:S(2)}) copy-start(f32[256]{0:T(256)S(1)} %broadcast_multiply_fusion.13) | copy-start | bytes 3076
  226.0 108.3 %copy-start.102 = (f32[256]{0:T(256)}, f32[256]{0:T(256)S(1)}, u32[]{:S(2)}) copy-start(f32[256]{0:T(256)S(1)} %add_rsqrt_fusion.1) | copy-start | bytes 3076
  229.0 24.9 %copy-start.62 = (bf16[256,512]{1,0:T(8,128)(2,1)}, bf16[256,512]{1,0:T(8,128)(2,1)S(1)}, u32[]{:S(2)}) copy-start(bf16[256,512]{1,0:T(8,128)(2,1)S(1)} %get-tuple-element.31) | copy-start | bytes 786436
  239.5 14.4 %copy-start.27 = (bf16[512,1024]{1,0:T(8,128)(2,1)S(1)}, bf16[512,1024]{1,0:T(8,128)(2,1)}, u32[]{:S(2)}) copy-start(bf16[512,1024]{1,0:T(8,128)(2,1)} %param.46) | copy-start | bytes 3145732
  261.1 11.2 %copy-start.132 = (f32[256,4096]{1,0:T(8,128)}, f32[256,4096]{1,0:T(8,128)S(1)}, u32[]{:S(2)}) copy-start(f32[256,4096]{1,0:T(8,128)S(1)} %fusion.14) | copy-start | bytes 12582916
  261.1 11.2 %copy-start.64 = (bf16[256,512]{1,0:T(8,128)(2,1)S(1)}, bf16[256,512]{1,0:T(8,128)(2,1)}, u32[]{:S(2)}) copy-start(bf16[256,512]{1,0:T(8,128)(2,1)} %get-tuple-element.33) | copy-start | bytes 786436
  276.5 23.3 %copy-start.30 = (f32[1,256,1024]{2,1,0:T(8,128)}, f32[1,256,1024]{2,1,0:T(8,128)S(1)}, u32[]{:S(2)}) copy-start(f32[1,256,1024]{2,1,0:T(8,128)S(1)} %get-tuple-element.51) | copy-start | bytes 3145732
  299.9 13.8 %slice-start.4 = ((s8[6291456]{0:T(1024)(128)(4,1)}), s8[2097152]{0:T(1024)(128)(4,1)S(1)}, s32[]{:S(2)}) async-start(s8[6291456]{0:T(1024)(128)(4,1)} %bitcast.474), calls=%async_computation.20 | async-start | bytes 4194304
  319.2 14.7 %copy-start.60 = (bf16[256,512]{1,0:T(8,128)(2,1)}, bf16[256,512]{1,0:T(8,128)(2,1)S(1)}, u32[]{:S(2)}) copy-start(bf16[256,512]{1,0:T(8,128)(2,1)S(1)} %get-tuple-element.97) | copy-start | bytes 786436
  320.2 77.6 %all-to-all-start.8 = ((f32[4,1,128]{2,1,0:T(1,128)}), f32[4,1,128]{2,1,0:T(1,128)S(1)}, u32[]{:S(2)}, u32[]{:S(2)}) async-start(f32[4,1,128]{2,1,0:T(1,128)} %reshape.1540), calls=%async_computation.8 | async-start | bytes 4096 | tf_op jit(solution)/shard_map/all_to_all | solution.py:35
  374.6 9.0 %copy-start.111 = (f32[256]{0:T(256)}, f32[256]{0:T(256)S(1)}, u32[]{:S(2)}) copy-start(f32[256]{0:T(256)S(1)} %broadcast_multiply_fusion.1) | copy-start | bytes 3076
  375.5 12.4 %slice-start.2 = ((s8[4718592]{0:T(1024)(128)(4,1)}), s8[524288]{0:T(1024)(128)(4,1)S(1)}, s32[]{:S(2)}) async-start(s8[4718592]{0:T(1024)(128)(4,1)} %bitcast.472), calls=%async_computation.18 | async-start | bytes 1048576
  383.6 11.4 %copy-start.25 = (f32[1,286,16,64]{1,3,2,0:T(8,128)}, f32[1,286,16,64]{1,3,2,0:T(8,128)S(1)}, u32[]{:S(2)}) copy-start(f32[1,286,16,64]{1,3,2,0:T(8,128)S(1)} %fusion.112) | copy-start | bytes 3514372
  397.7 8.9 %all-to-all-start.12 = ((f32[4,1,256]{2,1,0:T(1,128)}), f32[4,1,256]{2,1,0:T(1,128)S(1)}, u32[]{:S(2)}, u32[]{:S(2)}) async-start(f32[4,1,256]{2,1,0:T(1,128)} %reshape.1542), calls=%async_computation.12 | async-start | bytes 8192 | tf_op jit(solution)/shard_map/all_to_all | solution.py:35
  406.6 12.4 %all-to-all-start.4 = ((f32[4,1,15360]{2,1,0:T(1,128)}), f32[4,1,15360]{2,1,0:T(1,128)}, u32[]{:S(2)}, u32[]{:S(2)}) async-start(f32[4,1,15360]{2,1,0:T(1,128)} %reshape.1536), calls=%async_computation.4 | async-start | bytes 491520 | tf_op jit(solution)/shard_map/all_to_all | solution.py:35
  419.0 15.6 %all-to-all-start.9 = ((f32[32,1,4]{2,1,0:T(1,128)}), f32[32,1,4]{2,1,0:T(1,128)S(1)}, u32[]{:S(2)}, u32[]{:S(2)}) async-start(f32[32,1,4]{2,1,0:T(1,128)} %bitcast.206), calls=%async_computation.9 | async-start | bytes 32768 | tf_op jit(solution)/shard_map/all_to_all | solution.py:43
  435.2 13.5 %all-to-all-start.13 = ((f32[32,1,8]{2,1,0:T(1,128)}), f32[32,1,8]{2,1,0:T(1,128)}, u32[]{:S(2)}, u32[]{:S(2)}) async-start(f32[32,1,8]{2,1,0:T(1,128)} %copy.186), calls=%async_computation.13 | async-start | bytes 32768 | tf_op jit(solution)/shard_map/all_to_all | solution.py:43
  448.7 23.2 %all-to-all-start.5 = ((f32[32,1,480]{2,1,0:T(1,128)}), f32[32,1,480]{2,1,0:T(1,128)S(1)}, u32[]{:S(2)}, u32[]{:S(2)}) async-start(f32[32,1,480]{2,1,0:T(1,128)} %reshape.1538), calls=%async_computation.5 | async-start | bytes 131072 | tf_op jit(solution)/shard_map/all_to_all | solution.py:43
  471.9 27.6 %all-to-all-start.2 = ((bf16[16,2,12288]{2,1,0:T(2,128)(2,1)}), bf16[16,2,12288]{2,1,0:T(2,128)(2,1)}, u32[]{:S(2)}, u32[]{:S(2)}) async-start(bf16[16,2,12288]{2,1,0:T(2,128)(2,1)} %reshape.1534), calls=%async_computation.2 | async-start | bytes 1572864 | tf_op jit(solution)/shard_map/all_to_all | solution.py:338
  499.5 19.8 %all-to-all-start.3 = ((bf16[16,2,12288]{2,1,0:T(2,128)(2,1)}), bf16[16,2,12288]{2,1,0:T(2,128)(2,1)}, u32[]{:S(2)}, u32[]{:S(2)}) async-start(bf16[16,2,12288]{2,1,0:T(2,128)(2,1)} %reshape.1532), calls=%async_computation.3 | async-start | bytes 1572864 | tf_op jit(solution)/shard_map/all_to_all | solution.py:338
  519.3 28.7 %all-to-all-start.10 = ((f32[4,32,512,8]{2,3,1,0:T(8,128)}), f32[4,32,512,8]{2,3,1,0:T(8,128)}, u32[]{:S(2)}, u32[]{:S(2)}) async-start(f32[4,32,512,8]{2,3,1,0:T(8,128)} %copy.183), calls=%async_computation.10 | async-start | bytes 4194304 | tf_op jit(solution)/shard_map/all_to_all | solution.py:35
  548.0 27.5 %all-to-all-start.6 = ((f32[4,32,8,512]{3,2,1,0:T(8,128)}), f32[4,32,8,512]{3,2,1,0:T(8,128)}, u32[]{:S(2)}, u32[]{:S(2)}) async-start(f32[4,32,8,512]{3,2,1,0:T(8,128)} %bitcast.482), calls=%async_computation.6 | async-start | bytes 4194304 | tf_op jit(solution)/shard_map/all_to_all | solution.py:35
  552.5 9.4 %copy-start.5 = (bf16[16,256,286]{1,2,0:T(8,128)(2,1)S(1)}, bf16[16,256,286]{1,2,0:T(8,128)(2,1)}, u32[]{:S(2)}) copy-start(bf16[16,256,286]{1,2,0:T(8,128)(2,1)} %copy-done.4) | copy-start | bytes 7028740
  552.5 9.4 %copy-start.35 = (bf16[30,1024]{0,1:T(8,128)(2,1)S(1)}, bf16[30,1024]{0,1:T(8,128)(2,1)}, u32[]{:S(2)}) copy-start(bf16[30,1024]{0,1:T(8,128)(2,1)} %copy-done.34) | copy-start | bytes 184324
  552.5 9.4 %copy-start.42 = (bf16[1,256,1024]{1,2,0:T(8,128)(2,1)S(1)}, bf16[1,256,1024]{1,2,0:T(8,128)(2,1)}, u32[]{:S(2)}) copy-start(bf16[1,256,1024]{1,2,0:T(8,128)(2,1)} %copy-done.41) | copy-start | bytes 1572868
  564.2 21.7 %copy-start.10 = (f32[1,256,1024]{2,1,0:T(8,128)S(1)}, f32[1,256,1024]{2,1,0:T(8,128)}, u32[]{:S(2)}) copy-start(f32[1,256,1024]{2,1,0:T(8,128)} %copy-done.8) | copy-start | bytes 3145732
  564.2 21.7 %copy-start.67 = (bf16[16,64,256]{2,1,0:T(8,128)(2,1)S(1)}, bf16[16,64,256]{2,1,0:T(8,128)(2,1)}, u32[]{:S(2)}) copy-start(bf16[16,64,256]{2,1,0:T(8,128)(2,1)} %fusion.277) | copy-start | bytes 1572868
  564.2 21.7 %copy-start.87 = (f32[256]{0:T(256)S(1)}, f32[256]{0:T(256)}, u32[]{:S(2)}) copy-start(f32[256]{0:T(256)} %copy-done.85) | copy-start | bytes 3076
  564.3 21.7 %copy-start.93 = (f32[256]{0:T(256)S(1)}, f32[256]{0:T(256)}, u32[]{:S(2)}) copy-start(f32[256]{0:T(256)} %copy-done.91) | copy-start | bytes 3076
  564.3 21.7 %copy-start.112 = (f32[256]{0:T(256)S(1)}, f32[256]{0:T(256)}, u32[]{:S(2)}) copy-start(f32[256]{0:T(256)} %copy-done.111) | copy-start | bytes 3076
  564.3 21.7 %copy-start.114 = (f32[256]{0:T(256)S(1)}, f32[256]{0:T(256)}, u32[]{:S(2)}) copy-start(f32[256]{0:T(256)} %copy-done.113) | copy-start | bytes 3076
  575.5 21.4 %all-to-all-start.11 = ((f32[32,512,8]{1,2,0:T(8,128)}), f32[32,512,8]{1,2,0:T(8,128)S(1)}, u32[]{:S(2)}, u32[]{:S(2)}) async-start(f32[32,512,8]{1,2,0:T(8,128)} %reduce_sum.502), calls=%async_computation.11 | async-start | bytes 1048576 | tf_op jit(solution)/shard_map/all_to_all | solution.py:43
  592.1 12.4 %copy-start.83 = (f32[32,1,4]{2,1,0:T(1,128)S(1)}, f32[32,1,4]{2,1,0:T(1,128)}, u32[]{:S(2)}) copy-start(f32[32,1,4]{2,1,0:T(1,128)} %copy-done.82) | copy-start | bytes 1540
  596.9 10.3 %copy-start.51 = (f32[32,512,8]{1,2,0:T(8,128)}, f32[32,512,8]{1,2,0:T(8,128)S(1)}, u32[]{:S(2)}) copy-start(f32[32,512,8]{1,2,0:T(8,128)S(1)} %all-to-all-done.11) | copy-start | bytes 1572868
  596.9 22.4 %all-to-all-start.7 = ((f32[32,8,512]{2,1,0:T(8,128)}), f32[32,8,512]{2,1,0:T(8,128)}, u32[]{:S(2)}, u32[]{:S(2)}) async-start(f32[32,8,512]{2,1,0:T(8,128)} %reduce_sum.496), calls=%async_computation.7 | async-start | bytes 1048576 | tf_op jit(solution)/shard_map/all_to_all | solution.py:43
  (99 other events, 400.5 us)
Sparse Core Ops, SparseCore 0:
  17.9 123.9 all-gather.8
  143.5 50.6 all-gather.10
where the time goes:
time: 641 us; the launch traced here: 628 us
  matrix products  238 us (37%)
  local copies, waits for them, and re-layouts  89.4 us (14%)
  starting transfers between devices  87 us (14%)
  waiting for transfers between devices  83.9 us (13%)
  other arithmetic  59.3 us (9%)
  blocking collectives  54.3 us (8%)
  between operations  16.9 us (3%)
    dot_general x16, matrix products, back_product(): lax.dot_general(grad_in, weight_in, (((grad_in.ndim - 1,), (1,)), ((), ()...  89 us
    dot_general x18, matrix products, product(): return jnp.dot(left, right, preferred_element_type=jnp.float32)  73.8 us
    all_gather x1, waiting for transfers between devices, side_by_side(): lax.all_gather(both, axis, axis=dim, tiled=True)  51.3 us
    unnamed x317, local copies, waits for them, and re-layouts  47.2 us
    all_to_all x5, starting transfers between devices, sum_by_axis(): lax.all_to_all(nearer, far, split_axis=0, concat_axis=0, tiled=True)  35.7 us
    all_to_all x5, waiting for transfers between devices, sent_and_summed(): lax.all_to_all(tiles, axis, split_axis=0, concat_axis=0, tiled=True)  22.1 us
    all_to_all x5, starting transfers between devices, sent_and_summed(): lax.all_to_all(tiles, axis, split_axis=0, concat_axis=0, tiled=True)  21.7 us
    unnamed x8, other arithmetic  16.8 us
  transfers between devices with their start and end apart: 16, of which 7 were waited for; matrix products, arithmetic and copies ran while one was open for 45% of the time, Pallas kernels for 0%

commit v1 on v0

v1 whole, which is shorter than its diff:
```python
import functools

import jax
import jax.numpy as jnp
from jax import lax
from jax.experimental import pallas as pl
from jax.experimental.pallas import tpu as pltpu
from jax.sharding import Mesh
from jax.sharding import PartitionSpec as P

HEAD_DIM = 64
PAIR = 128
GROUP = 256
PREFIX_PAD = 32
MEM = ("mem_0", "mem_1")
DP = ("dp_0", "dp_1")
DP_MEM = ("dp_0", "dp_1", "mem_0", "mem_1")

NEGATIVE = -1e30
EPSILON = 1e-05
SCALE = HEAD_DIM ** (-0.5)
BF = jnp.bfloat16
F32 = jnp.float32
VMEM_BYTES = 60 * 1024 * 1024


def dot_nn(left, right):
    return lax.dot_general(left, right, (((1,), (0,)), ((), ())), preferred_element_type=F32)


def dot_nt(left, right):
    return lax.dot_general(left, right, (((1,), (1,)), ((), ())), preferred_element_type=F32)


def dot_tn(left, right):
    return lax.dot_general(left, right, (((0,), (0,)), ((), ())), preferred_element_type=F32)


def head_masks():
    lane = lax.broadcasted_iota(jnp.int32, (1, PAIR), 1)
    return [jnp.where((lane >= HEAD_DIM) == bool(h), 1.0, 0.0).astype(BF) for h in range(2)]


def norm_stats(hidden):
    centred = hidden - jnp.mean(hidden, axis=-1, keepdims=True)
    inverse = lax.rsqrt(jnp.mean(centred * centred, axis=-1, keepdims=True) + EPSILON)
    return centred * inverse, inverse


def norm_back(grad_in, normed, inverse, gain):
    scaled = grad_in * gain
    return inverse * (
        scaled
        - jnp.mean(scaled, axis=-1, keepdims=True)
        - normed * jnp.mean(scaled * normed, axis=-1, keepdims=True)
    )


def gelu_both(pre):
    cdf = 0.5 * (1.0 + lax.erf(pre * (0.5**0.5)))
    density = jnp.exp(-0.5 * pre * pre) * 0.3989422804014327
    return pre * cdf, cdf + pre * density


def self_forward_kernel(
    len_ref, tok_ref, wq_ref, wk_ref, wv_ref, pk_ref, pv_ref, wo_ref, wcq_ref, norm_ref,
    q_ref, k_ref, v_ref, nrm_ref, inv_ref, cq_ref, att_ref,
):
    step = pl.program_id(0)
    seqs = len_ref.shape[0]
    rows_all = tok_ref.shape[0]
    tgt = rows_all // seqs
    tok = tok_ref[...]
    q_ref[...] = dot_nn(tok, wq_ref[...]).astype(BF)
    k_ref[...] = dot_nn(tok, wk_ref[...]).astype(BF)
    v_ref[...] = dot_nn(tok, wv_ref[...]).astype(BF)
    masks = head_masks()
    row = lax.broadcasted_iota(jnp.int32, (tgt, tgt), 0)
    col = lax.broadcasted_iota(jnp.int32, (tgt, tgt), 1)
    slot = lax.broadcasted_iota(jnp.int32, (tgt, PREFIX_PAD), 1)
    for s in range(seqs):
        visible = (col <= row) & (col < len_ref[s])
        for p in range(GROUP // PAIR):
            at = pl.ds(p * PAIR, PAIR)
            here = pl.ds(s * tgt, tgt)
            q = q_ref[here, at] * SCALE
            k = k_ref[here, at]
            v = v_ref[here, at]
            pk = pk_ref[:, at]
            pv = pv_ref[:, at]
            total = jnp.zeros((tgt, PAIR), F32)
            for mask in masks:
                s1 = jnp.where(visible, dot_nt(q, k * mask), NEGATIVE)
                s0 = jnp.where(slot < 30, dot_nt(q, pk * mask), NEGATIVE)
                top = jnp.maximum(
                    jnp.max(s1, axis=1, keepdims=True), jnp.max(s0, axis=1, keepdims=True)
                )
                e1 = jnp.exp(s1 - top)
                e0 = jnp.exp(s0 - top)
                inv = 1.0 / (
                    jnp.sum(e1, axis=1, keepdims=True) + jnp.sum(e0, axis=1, keepdims=True)
                )
                out = dot_nn((e1 * inv).astype(BF), v * mask) + dot_nn(
                    (e0 * inv).astype(BF), pv * mask
                )
                total = total + out
            att_ref[here, pl.ds(pl.multiple_of(step * GROUP + p * PAIR, PAIR), PAIR)] = (
                total.astype(BF)
            )

    @pl.when(step == pl.num_programs(0) - 1)
    def _():
        hidden = tok.astype(F32) + dot_nn(att_ref[...], wo_ref[...])
        nrm, inv = norm_stats(hidden)
        nrm_ref[...] = nrm
        inv_ref[...] = inv
        first = nrm * norm_ref[0:1, :] + norm_ref[1:2, :]
        cq_ref[...] = dot_nn(first.astype(BF), wcq_ref[...]).astype(BF)


def cross_forward_kernel(
    len_ref, mem_ref, wk_ref, wv_ref, cq_ref, wco_ref, nrm1_ref, norm_ref,
    mk_ref, mv_ref, nrm_ref, inv_ref, att_ref,
):
    step = pl.program_id(0)
    seqs = len_ref.shape[0]
    tgt = cq_ref.shape[0] // seqs
    src = mem_ref.shape[0] // seqs
    mem = mem_ref[...]
    mk_ref[...] = dot_nn(mem, wk_ref[...]).astype(BF)
    mv_ref[...] = dot_nn(mem, wv_ref[...]).astype(BF)
    masks = head_masks()
    slot = lax.broadcasted_iota(jnp.int32, (tgt, src), 1)
    for s in range(seqs):
        valid = slot < len_ref[s]
        for p in range(GROUP // PAIR):
            at = pl.ds(p * PAIR, PAIR)
            here = pl.ds(s * tgt, tgt)
            there = pl.ds(s * src, src)
            q = cq_ref[here, at] * SCALE
            k = mk_ref[there, at]
            v = mv_ref[there, at]
            total = jnp.zeros((tgt, PAIR), F32)
            for mask in masks:
                sc = jnp.where(valid, dot_nt(q, k * mask), NEGATIVE)
                e = jnp.exp(sc - jnp.max(sc, axis=1, keepdims=True))
                inv = 1.0 / jnp.sum(e, axis=1, keepdims=True)
                total = total + dot_nn(e.astype(BF), v * mask) * inv
            att_ref[here, pl.ds(pl.multiple_of(step * GROUP + p * PAIR, PAIR), PAIR)] = (
                total.astype(BF)
            )

    @pl.when(step == pl.num_programs(0) - 1)
    def _():
        first = nrm1_ref[...] * norm_ref[0:1, :] + norm_ref[1:2, :]
        nrm, inv = norm_stats(first + dot_nn(att_ref[...], wco_ref[...]))
        nrm_ref[...] = nrm
        inv_ref[...] = inv


def ffn_kernel(
    len_ref, nrm2_ref, inv2_ref, cot_ref, win_ref, wff_ref, down_ref, db_ref, up_ref, ub_ref,
    norm_ref,
    out_ref, gtwo_ref, dw_ref, db_out_ref, uw_ref, ub_out_ref,
    acc_ref, low_ref, slope_ref, aact_ref, aslope_ref, g_ref,
):
    phase = pl.program_id(0)
    j = pl.program_id(1)
    last = pl.num_programs(1) - 1
    seqs = len_ref.shape[0]
    rows_all = nrm2_ref.shape[0]
    tgt = rows_all // seqs
    half = rows_all // 2

    @pl.when((phase == 0) & (j == 0))
    def _():
        for b in range(2):
            r = pl.ds(b * half, half)
            second = nrm2_ref[r, :] * norm_ref[2:3, :] + norm_ref[3:4, :]
            low = second.astype(BF)
            low_ref[r, :] = low
            act, slope = gelu_both(dot_nn(low, down_ref[...]) + db_ref[...])
            act = act.astype(BF)
            aact_ref[r, :] = act
            aslope_ref[r, :] = slope.astype(BF)
            acc_ref[r, :] = second + 4.0 * (dot_nn(act, up_ref[...]) + ub_ref[...])

    @pl.when(phase == 0)
    def _():
        for b in range(2):
            r = pl.ds(b * half, half)
            act, slope = gelu_both(dot_nn(low_ref[r, :], win_ref[...]))
            slope_ref[j, r, :] = slope.astype(BF)
            acc_ref[r, :] += dot_nn(act.astype(BF), wff_ref[...])

    @pl.when((phase == 1) & (j == 0))
    def _():
        for s in range(seqs):
            r = pl.ds(s * tgt, tgt)
            nrm, inv = norm_stats(acc_ref[r, :])
            out_ref[r, :] = (nrm * norm_ref[4:5, :] + norm_ref[5:6, :]).astype(BF)
            live = lax.broadcasted_iota(jnp.int32, (tgt, 1), 0) < len_ref[s]
            go = jnp.where(live, cot_ref[r, :].astype(F32), 0.0)
            gthree = norm_back(go, nrm, inv, norm_ref[4:5, :])
            g_ref[r, :] = gthree.astype(BF)
            acc_ref[r, :] = gthree
        agrad = g_ref[...] * 4.0
        ub_out_ref[...] = jnp.sum(agrad.astype(F32), axis=0, keepdims=True)
        uw_ref[...] = dot_tn(agrad, aact_ref[...]).astype(BF)
        apg = (dot_nt(agrad, up_ref[...]) * aslope_ref[...].astype(F32)).astype(BF)
        db_out_ref[...] = jnp.sum(apg.astype(F32), axis=0, keepdims=True)
        dw_ref[...] = dot_tn(low_ref[...], apg).astype(BF)
        acc_ref[...] += dot_nt(apg, down_ref[...])

    @pl.when(phase == 1)
    def _():
        for b in range(2):
            r = pl.ds(b * half, half)
            grad = (dot_nt(g_ref[r, :], wff_ref[...]) * slope_ref[j, r, :].astype(F32)).astype(BF)
            acc_ref[r, :] += dot_nt(grad, win_ref[...])

    @pl.when((phase == 1) & (j == last))
    def _():
        gtwo_ref[...] = norm_back(acc_ref[...], nrm2_ref[...], inv2_ref[...], norm_ref[2:3, :])


def cross_backward_kernel(
    len_ref, gtwo_ref, wco_ref, cq_ref, mk_ref, mv_ref, wk_ref, wv_ref,
    dq_ref, dmem_ref, low_ref, acc_ref, dk_ref, dv_ref,
):
    step = pl.program_id(0)
    seqs = len_ref.shape[0]
    tgt = cq_ref.shape[0] // seqs
    src = mk_ref.shape[0] // seqs

    @pl.when(step == 0)
    def _():
        low_ref[...] = gtwo_ref[...].astype(BF)
        acc_ref[...] = jnp.zeros_like(acc_ref)

    mg_all = dot_nt(low_ref[...], wco_ref[...]).astype(BF)
    masks = head_masks()
    slot = lax.broadcasted_iota(jnp.int32, (src, tgt), 0)
    for s in range(seqs):
        valid = slot < len_ref[s]
        for p in range(GROUP // PAIR):
            at = pl.ds(p * PAIR, PAIR)
            here = pl.ds(s * tgt, tgt)
            there = pl.ds(s * src, src)
            q = cq_ref[here, at] * SCALE
            k = mk_ref[there, at]
            v = mv_ref[there, at]
            mg = mg_all[s * tgt : (s + 1) * tgt, p * PAIR : (p + 1) * PAIR]
            dq = jnp.zeros((tgt, PAIR), F32)
            dk = jnp.zeros((src, PAIR), F32)
            dv = jnp.zeros((src, PAIR), F32)
            for mask in masks:
                km = k * mask
                sc = jnp.where(valid, dot_nt(km, q), NEGATIVE)
                e = jnp.exp(sc - jnp.max(sc, axis=0, keepdims=True))
                prob = e * (1.0 / jnp.sum(e, axis=0, keepdims=True))
                dprob = dot_nt(v * mask, mg)
                delta = jnp.sum(prob * dprob, axis=0, keepdims=True)
                ds = (prob * (dprob - delta)).astype(BF)
                dq = dq + dot_tn(ds, km)
                dk = dk + dot_nn(ds, q * mask)
                dv = dv + dot_nn(prob.astype(BF), mg * mask)
            dq_ref[here, at] = (dq * SCALE).astype(BF)
            dk_ref[there, at] = dk.astype(BF)
            dv_ref[there, at] = dv.astype(BF)
    acc_ref[...] += dot_nt(dk_ref[...], wk_ref[...]) + dot_nt(dv_ref[...], wv_ref[...])

    @pl.when(step == pl.num_programs(0) - 1)
    def _():
        dmem_ref[...] = acc_ref[...].astype(BF)


def self_backward_kernel(
    len_ref, gtwo_ref, cdq_ref, wcq_ref, nrm1_ref, inv1_ref, norm_ref,
    wo_ref, q_ref, k_ref, v_ref, pk_ref, pv_ref, wq_ref, wk_ref, wv_ref,
    din_ref, dpk_ref, dpv_ref, low_ref, acc_ref, dq_ref, dk_ref, dv_ref,
):
    step = pl.program_id(0)
    seqs = len_ref.shape[0]
    tgt = gtwo_ref.shape[0] // seqs

    @pl.when(step == 0)
    def _():
        grad_first = gtwo_ref[...] + dot_nt(cdq_ref[...], wcq_ref[...])
        grad_one = norm_back(grad_first, nrm1_ref[...], inv1_ref[...], norm_ref[0:1, :])
        acc_ref[...] = grad_one
        low_ref[...] = grad_one.astype(BF)

    ag_all = dot_nt(low_ref[...], wo_ref[...]).astype(BF)
    masks = head_masks()
    row = lax.broadcasted_iota(jnp.int32, (tgt, tgt), 1)
    col = lax.broadcasted_iota(jnp.int32, (tgt, tgt), 0)
    slot = lax.broadcasted_iota(jnp.int32, (PREFIX_PAD, tgt), 0)
    for p in range(GROUP // PAIR):
        at = pl.ds(p * PAIR, PAIR)
        pk = pk_ref[:, at]
        pv = pv_ref[:, at]
        dpk = jnp.zeros((PREFIX_PAD, PAIR), F32)
        dpv = jnp.zeros((PREFIX_PAD, PAIR), F32)
        for s in range(seqs):
            visible = (col <= row) & (col < len_ref[s])
            here = pl.ds(s * tgt, tgt)
            q = q_ref[here, at] * SCALE
            k = k_ref[here, at]
            v = v_ref[here, at]
            ag = ag_all[s * tgt : (s + 1) * tgt, p * PAIR : (p + 1) * PAIR]
            dq = jnp.zeros((tgt, PAIR), F32)
            dk = jnp.zeros((tgt, PAIR), F32)
            dv = jnp.zeros((tgt, PAIR), F32)
            for mask in masks:
                km = k * mask
                pkm = pk * mask
                qm = q * mask
                agm = ag * mask
                s1 = jnp.where(visible, dot_nt(km, q), NEGATIVE)
                s0 = jnp.where(slot < 30, dot_nt(pkm, q), NEGATIVE)
                top = jnp.maximum(
                    jnp.max(s1, axis=0, keepdims=True), jnp.max(s0, axis=0, keepdims=True)
                )
                e1 = jnp.exp(s1 - top)
                e0 = jnp.exp(s0 - top)
                inv = 1.0 / (
                    jnp.sum(e1, axis=0, keepdims=True) + jnp.sum(e0, axis=0, keepdims=True)
                )
                p1 = e1 * inv
                p0 = e0 * inv
                d1 = dot_nt(v * mask, ag)
                d0 = dot_nt(pv * mask, ag)
                delta = jnp.sum(p1 * d1, axis=0, keepdims=True) + jnp.sum(
                    p0 * d0, axis=0, keepdims=True
                )
                g1 = (p1 * (d1 - delta)).astype(BF)
                g0 = (p0 * (d0 - delta)).astype(BF)
                dq = dq + dot_tn(g1, km) + dot_tn(g0, pkm)
                dk = dk + dot_nn(g1, qm)
                dv = dv + dot_nn(p1.astype(BF), agm)
                dpk = dpk + dot_nn(g0, qm)
                dpv = dpv + dot_nn(p0.astype(BF), agm)
            dq_ref[here, at] = (dq * SCALE).astype(BF)
            dk_ref[here, at] = dk.astype(BF)
            dv_ref[here, at] = dv.astype(BF)
        dpk_ref[:, at] = dpk
        dpv_ref[:, at] = dpv
    acc_ref[...] += (
        dot_nt(dq_ref[...], wq_ref[...])
        + dot_nt(dk_ref[...], wk_ref[...])
        + dot_nt(dv_ref[...], wv_ref[...])
    )

    @pl.when(step == pl.num_programs(0) - 1)
    def _():
        din_ref[...] = acc_ref[...].astype(BF)


def whole(shape):
    return pl.BlockSpec(shape, lambda *_: (0,) * len(shape))


def columns(rows, width, offset=0):
    return pl.BlockSpec((rows, width), lambda i, *_: (0, i + offset))


def rows_of(height, width):
    return pl.BlockSpec((height, width), lambda i, *_: (i, 0))


def shaped(shape, dtype):
    return jax.ShapeDtypeStruct(shape, dtype)


def call(kernel, grid, in_specs, out_specs, outs, scratch, flops, moved, *args):
    return pl.pallas_call(
        kernel,
        grid_spec=pltpu.PrefetchScalarGridSpec(
            num_scalar_prefetch=1,
            grid=grid,
            in_specs=in_specs,
            out_specs=out_specs,
            scratch_shapes=scratch,
        ),
        out_shape=outs,
        compiler_params=pltpu.CompilerParams(
            vmem_limit_bytes=VMEM_BYTES,
            dimension_semantics=("arbitrary",) * len(grid),
        ),
        cost_estimate=pl.CostEstimate(flops=flops, bytes_accessed=moved, transcendentals=0),
    )(*args)


def self_forward(lens, tok, w_qkv, pk, pv, w_out, w_cq, norms):
    rows, width = tok.shape
    steps = width // GROUP
    return call(
        self_forward_kernel,
        (steps,),
        [
            whole((rows, width)),
            columns(width, GROUP),
            columns(width, GROUP, steps),
            columns(width, GROUP, 2 * steps),
            columns(PREFIX_PAD, GROUP),
            columns(PREFIX_PAD, GROUP),
            whole((width, width)),
            whole((width, width)),
            whole(norms.shape),
        ],
        [columns(rows, GROUP)] * 3
        + [whole((rows, width)), whole((rows, 1)), whole((rows, width))],
        [shaped((rows, width), BF)] * 3
        + [shaped((rows, width), F32), shaped((rows, 1), F32), shaped((rows, width), BF)],
        [pltpu.VMEM((rows, width), BF)],
        2 * rows * width * width * 5,
        20 * width * width,
        lens, tok, w_qkv, w_qkv, w_qkv, pk, pv, w_out, w_cq, norms,
    )


def cross_forward(lens, mem, w_ckv, cq, w_cout, nrm1, norms):
    rows, width = cq.shape
    steps = width // GROUP
    places = mem.shape[0]
    return call(
        cross_forward_kernel,
        (steps,),
        [
            whole((places, width)),
            columns(width, GROUP),
            columns(width, GROUP, steps),
            columns(rows, GROUP),
            whole((width, width)),
            whole((rows, width)),
            whole(norms.shape),
        ],
        [columns(places, GROUP)] * 2 + [whole((rows, width)), whole((rows, 1))],
        [shaped((places, width), BF)] * 2 + [shaped((rows, width), F32), shaped((rows, 1), F32)],
        [pltpu.VMEM((rows, width), BF)],
        2 * width * width * (rows + 2 * places),
        14 * width * width,
        lens, mem, w_ckv, w_ckv, cq, w_cout, nrm1, norms,
    )


def ffn(lens, nrm2, inv2, cot, w_in, w_ff, down, db, up, ub, norms):
    rows, width = nrm2.shape
    hidden = w_in.shape[1]
    adapt = down.shape[1]
    block = 512
    steps = hidden // block
    return call(
        ffn_kernel,
        (2, steps),
        [
            whole((rows, width)),
            whole((rows, 1)),
            whole((rows, width)),
            pl.BlockSpec((width, block), lambda p, j, *_: (0, j)),
            pl.BlockSpec((block, width), lambda p, j, *_: (j, 0)),
            whole((width, adapt)),
            whole((1, adapt)),
            whole((adapt, width)),
            whole((1, width)),
            whole(norms.shape),
        ],
        [
            whole((rows, width)),
            whole((rows, width)),
            whole((width, adapt)),
            whole((1, adapt)),
            whole((width, adapt)),
            whole((1, width)),
        ],
        [
            shaped((rows, width), BF),
            shaped((rows, width), F32),
            shaped((width, adapt), BF),
            shaped((1, adapt), F32),
            shaped((width, adapt), BF),
            shaped((1, width), F32),
        ],
        [
            pltpu.VMEM((rows, width), F32),
            pltpu.VMEM((rows, width), BF),
            pltpu.VMEM((steps, rows, block), BF),
            pltpu.VMEM((rows, adapt), BF),
            pltpu.VMEM((rows, adapt), BF),
            pltpu.VMEM((rows, width), BF),
        ],
        2 * rows * width * (4 * hidden + 6 * adapt),
        8 * width * hidden,
        lens, nrm2, inv2, cot, w_in, w_ff, down, db, up, ub, norms,
    )


def cross_backward(lens, gtwo, w_cout, cq, mk, mv, w_ckv):
    rows, width = cq.shape
    steps = width // GROUP
    places = mk.shape[0]
    return call(
        cross_backward_kernel,
        (steps,),
        [
            whole((rows, width)),
            rows_of(GROUP, width),
            columns(rows, GROUP),
            columns(places, GROUP),
            columns(places, GROUP),
            columns(width, GROUP),
            columns(width, GROUP, steps),
        ],
        [columns(rows, GROUP), whole((places, width))],
        [shaped((rows, width), BF), shaped((places, width), BF)],
        [
            pltpu.VMEM((rows, width), BF),
            pltpu.VMEM((places, width), F32),
            pltpu.VMEM((places, GROUP), BF),
            pltpu.VMEM((places, GROUP), BF),
        ],
        2 * width * width * (rows + 2 * places),
        14 * width * width,
        lens, gtwo, w_cout, cq, mk, mv, w_ckv, w_ckv,
    )


def self_backward(
    lens, gtwo, cdq, w_cq, nrm1, inv1, norms, w_out, q, k, v, pk, pv, w_qkv
):
    rows, width = q.shape
    steps = width // GROUP
    return call(
        self_backward_kernel,
        (steps,),
        [
            whole((rows, width)),
            whole((rows, width)),
            whole((width, width)),
            whole((rows, width)),
            whole((rows, 1)),
            whole(norms.shape),
            rows_of(GROUP, width),
            columns(rows, GROUP),
            columns(rows, GROUP),
            columns(rows, GROUP),
            columns(PREFIX_PAD, GROUP),
            columns(PREFIX_PAD, GROUP),
            columns(width, GROUP),
            columns(width, GROUP, steps),
            columns(width, GROUP, 2 * steps),
        ],
        [whole((rows, width)), columns(PREFIX_PAD, GROUP), columns(PREFIX_PAD, GROUP)],
        [
            shaped((rows, width), BF),
            shaped((PREFIX_PAD, width), F32),
            shaped((PREFIX_PAD, width), F32),
        ],
        [
            pltpu.VMEM((rows, width), BF),
            pltpu.VMEM((rows, width), F32),
            pltpu.VMEM((rows, GROUP), BF),
            pltpu.VMEM((rows, GROUP), BF),
            pltpu.VMEM((rows, GROUP), BF),
        ],
        2 * rows * width * width * 5,
        20 * width * width,
        lens, gtwo, cdq, w_cq, nrm1, inv1, norms, w_out, q, k, v, pk, pv, w_qkv, w_qkv, w_qkv,
    )


def local(
    tokens, memory, cotangent, tgt_len, src_len,
    self_qkv, self_out, cross_q, cross_kv, cross_out, ffn_in, ffn_out,
    first_gain, first_bias, second_gain, second_bias, third_gain, third_bias,
    prefix_key, prefix_value, down_weight, down_bias, up_weight, up_bias,
):
    mem_groups = lax.axis_size(MEM)
    mem_place = lax.axis_index(MEM)
    seqs, tgt, width = tokens.shape
    src_block = memory.shape[1]
    prefix = prefix_key.shape[0]

    def gathered(w):
        return lax.all_gather(w, DP, axis=0, tiled=True)

    vectors = jnp.stack(
        [first_gain, first_bias, second_gain, second_bias, third_gain, third_bias]
        + [third_bias] * 2
    )
    norms = lax.all_gather(vectors, DP, axis=1, tiled=True).astype(F32)
    w_qkv = gathered(self_qkv)
    w_oq = gathered(jnp.concatenate([self_out, cross_q], axis=1))
    w_out, w_cq = w_oq[:, :width], w_oq[:, width:]
    w_ckv = gathered(cross_kv)
    w_cout = gathered(cross_out)
    w_in = gathered(ffn_in)
    w_ff = gathered(ffn_out)

    mem_rows = lax.all_to_all(memory, MEM, split_axis=0, concat_axis=1, tiled=True)
    mem_rows = mem_rows.reshape(-1, width)
    own_src = lax.dynamic_slice_in_dim(src_len, mem_place * seqs, seqs, 0)

    tok = tokens.reshape(seqs * tgt, width)
    cot = cotangent.reshape(seqs * tgt, width)
    pk = jnp.pad(prefix_key, ((0, PREFIX_PAD - prefix), (0, 0)))
    pv = jnp.pad(prefix_value, ((0, PREFIX_PAD - prefix), (0, 0)))

    q, k, v, nrm1, inv1, cq = self_forward(tgt_len, tok, w_qkv, pk, pv, w_out, w_cq, norms)
    mk, mv, nrm2, inv2 = cross_forward(own_src, mem_rows, w_ckv, cq, w_cout, nrm1, norms)
    output, gtwo, dw, db, uw, ub = ffn(
        tgt_len, nrm2, inv2, cot, w_in, w_ff,
        down_weight, down_bias.astype(F32)[None], up_weight, up_bias.astype(F32)[None], norms,
    )
    cdq, dmem = cross_backward(own_src, gtwo, w_cout, cq, mk, mv, w_ckv)
    memory_grad = lax.all_to_all(
        dmem.reshape(seqs, mem_groups * src_block, width),
        MEM, split_axis=1, concat_axis=0, tiled=True,
    )
    din, dpk, dpv = self_backward(
        tgt_len, gtwo, cdq, w_cq, nrm1, inv1, norms, w_out, q, k, v, pk, pv, w_qkv
    )

    ranks = mem_groups * lax.axis_size(DP)

    def summed(x):
        arrived = lax.all_to_all(x, DP_MEM, split_axis=0, concat_axis=0, tiled=True)
        return jnp.sum(arrived.astype(F32), axis=0)

    def blocks(x):
        return jnp.moveaxis(x.reshape(x.shape[0], ranks, -1), 1, 0)

    adapter = summed(
        jnp.concatenate(
            [dw.reshape(ranks, -1, dw.shape[1]), uw.reshape(ranks, -1, uw.shape[1])], axis=1
        )
    )
    high = dw.shape[0] // ranks
    small = [blocks(x) for x in (dpk[:prefix], dpv[:prefix], db, ub)]
    total = summed(jnp.concatenate([x.reshape(ranks, -1) for x in small], axis=1))
    parts = []
    start = 0
    for x in small:
        size = x.shape[1] * x.shape[2]
        parts.append(total[start : start + size].reshape(x.shape[1:]))
        start += size
    return (
        output.reshape(tokens.shape),
        din.reshape(tokens.shape),
        memory_grad,
        parts[0],
        parts[1],
        adapter[:high],
        parts[2][0],
        adapter[high:].T,
        parts[3][0],
    )


def solution(mesh):
    torus = Mesh(mesh.devices.reshape(4, 2, 4, 4), ("dp_0", "dp_1", "mem_0", "mem_1"))
    by_dp = P(DP, None)
    copied = P(None)
    return jax.shard_map(
        local,
        mesh=torus,
        in_specs=(
            P(DP_MEM, None, None), P(DP, MEM, None), P(DP_MEM, None, None), P(DP_MEM), P(DP),
            by_dp, by_dp, by_dp, by_dp, by_dp, by_dp, by_dp,
            P(DP), P(DP), P(DP), P(DP), P(DP), P(DP),
            copied, copied, copied, copied, copied, copied,
        ),
        out_specs=(
            P(DP_MEM, None, None),
            P(DP_MEM, None, None),
            P(DP, MEM, None),
            P(None, DP_MEM),
            P(None, DP_MEM),
            P(DP_MEM, None),
            P(DP_MEM),
            P(None, DP_MEM),
            P(DP_MEM),
        ),
        check_vma=False,
    )
```

time: 641 us -> 455 us (0.71)
  the two profiles are of different devices: /device:TPU:1 before, /device:TPU:0 now
where the time goes in v1:
time: 455 us; the launch traced here: 446 us
  waiting for transfers between devices  218 us (48%)
  Pallas kernels  145 us (32%)
  starting transfers between devices  25.6 us (6%)
  local copies, waits for them, and re-layouts  22.6 us (5%)
  between operations  14.9 us (3%)
  blocking collectives  11.9 us (3%)
  other arithmetic  8.56 us (2%)
    all_gather x6, waiting for transfers between devices, gathered(): return lax.all_gather(w, DP, axis=0, tiled=True)  152 us
    pallas_call x5, Pallas kernels, call(): pl.pallas_call(kernel, grid_spec=pltpu.PrefetchScalarGridSpec(num_scalar_...  145 us
    all_to_all x2, waiting for transfers between devices, summed(): arrived = lax.all_to_all(x, DP_MEM, split_axis=0, concat_axis=0, tiled=True)  31.8 us
    all_to_all x1, waiting for transfers between devices, local(): lax.all_to_all(dmem.reshape(seqs, mem_groups * src_block, width), MEM, sp...  22.5 us
    all_to_all x2, starting transfers between devices, summed(): arrived = lax.all_to_all(x, DP_MEM, split_axis=0, concat_axis=0, tiled=True)  13.5 us
    all_gather x1, blocking collectives, local(): norms = lax.all_gather(vectors, DP, axis=1, tiled=True).astype(F32)  11.9 us
  transfers between devices with their start and end apart: 10, of which 8 were waited for; matrix products, arithmetic and copies ran while one was open for 5% of the time, Pallas kernels for 11%

profile of v1, /device:TPU:0, one launch (start us, length us, event | category | flops | bytes accessed | tf_op | source)
XLA Modules:
  0.0 446.4 jit_solution(8082483044252364231)
XLA Ops:
  7.2 0.0 all-gather.11.cloned.1.call-start
  7.2 1.9 pad_maximum_fusion.1
  9.1 0.0 all-gather.9.cloned.1.call-start
  9.2 0.7 all-gather.9.cloned.1.call-update
  9.9 0.0 all-gather.13.cloned.1.call-start
  9.9 0.7 all-gather.13.cloned.1.call-update
  10.6 0.0 all-gather.7.cloned.1.call-start
  10.6 0.5 all-gather.7.cloned.1.call-update
  11.2 0.0 all-gather.15.cloned.1.call-start
  11.2 0.5 all-gather.15.cloned.1.call-update
  11.9 0.0 all-gather.17.cloned.1.call-start
  11.9 0.5 all-gather.17.cloned.1.call-update
  12.5 8.1 %all-to-all-start = ((bf16[32,24,1024]{2,1,0:T(8,128)(2,1)}), bf16[32,24,1024]{2,1,0:T(8,128)(2,1)S(1)}, u32[]{:S(2)}, u32[]{:S(2)}) async-start(bf16[32,24,1024]{2,1,0:T(8,128)(2,1)} %param.25), calls=%async_computation | async-start | bytes 3145728 | tf_op jit(solution)/shard_map/all_to_all | solution.py:601
  20.7 11.9 %all_gather.24 = bf16[8,1024]{1,0:T(8,128)(2,1)S(1)} all-gather(bf16[8,128]{1,0:T(8,128)(2,1)S(1)} %stack.29), channel_id=1, replica_groups=mesh['dp_0'=4,'dp_1'=2,'mem_0'=4,'mem_1'=4] {'dp_0','dp_1'}, dimensions={1}, use_global_device_ids=true | all-gather | bytes 18432 | tf_op jit(solution)/shard_map/all_gather | solution.py:592
  32.7 0.6 convert_element_type.11.norm_ref
  33.3 0.6 pad.7.pk_ref
  33.9 0.6 pad.8.pv_ref
  34.6 0.6 broadcast_in_dim.15
  35.2 0.6 broadcast_in_dim.14
  35.7 0.6 dynamic_slice.3.len_ref
  36.3 8.8 %all-to-all-done = bf16[32,24,1024]{2,1,0:T(8,128)(2,1)S(1)} async-done(((bf16[32,24,1024]{2,1,0:T(8,128)(2,1)}), bf16[32,24,1024]{2,1,0:T(8,128)(2,1)S(1)}, u32[]{:S(2)}, u32[]{:S(2)}) %all-to-all-start) | async-done | bytes 1572896 | tf_op jit(solution)/shard_map/all_to_all | solution.py:601
  45.1 1.3 copy.45
  46.4 4.6 %fusion = (bf16[1024,1024]{1,0:T(8,128)(2,1)}, bf16[1024,1024]{1,0:T(8,128)(2,1)}) fusion(bf16[1024,2048]{1,0:T(8,128)(2,1)} %all-gather.11.cloned.1.call-done), kind=kLoop, calls=%fused_computation.5 | loop fusion | bytes 8388608 | tf_op jit(solution)/shard_map/slice | solution.py:595
  51.0 36.4 %all-gather.9.cloned.1.call-done.wq_ref.wk_ref.wv_ref = bf16[1024,3072]{1,0:T(8,128)(2,1)} async-done(((bf16[128,3072]{1,0:T(8,128)(2,1)}), bf16[1024,3072]{1,0:T(8,128)(2,1)}) %all-gather.9.cloned.1.call-update) | async-done | bytes 6291472 | tf_op jit(solution)/shard_map/all_gather | solution.py:586
  87.4 27.7 %shard_map.295 = (bf16[512,1024]{1,0:T(8,128)(2,1)}, bf16[512,1024]{1,0:T(8,128)(2,1)}, bf16[512,1024]{1,0:T(8,128)(2,1)}, f32[512,1024]{1,0:T(8,128)}, f32[512,1]{1,0:T(8,128)}, /*index=5*/bf16[512,1024]{1,0:T(8,128)(2,1)}) custom-call(s32[2]{0:T(128)} %len_ref.5, bf16[512,1024]{1,0:T(8,128)(2,1)} %bitcast.46, ...), custom_call_target="tpu_custom_call" | custom-call | flops 5368709120 | bytes 20971520 | tf_op jit(solution)/shard_map/pallas_call | solution.py:377
  115.1 0.0 all-gather.13.cloned.1.call-done.wco_ref
  115.2 33.4 %all-gather.7.cloned.1.call-done.wk_ref.wv_ref = bf16[1024,2048]{1,0:T(8,128)(2,1)} async-done(((bf16[128,2048]{1,0:T(8,128)(2,1)}), bf16[1024,2048]{1,0:T(8,128)(2,1)}) %all-gather.7.cloned.1.call-update) | async-done | bytes 4194320 | tf_op jit(solution)/shard_map/all_gather | solution.py:586
  148.6 21.1 %shard_map.296 = (bf16[768,1024]{1,0:T(8,128)(2,1)}, bf16[768,1024]{1,0:T(8,128)(2,1)}, f32[512,1024]{1,0:T(8,128)}, f32[512,1]{1,0:T(8,128)}) custom-call(s32[2]{0:T(128)} %dynamic_slice.3.len_ref, bf16[768,1024]{1,0:T(8,128)(2,1)} %bitcast.43, bf16[1024,2048]{1,0:T(8,128)(2,1)} %all-gather.7.cloned.1.call-done.wk_ref.wv_ref, ...), custom_call_target="tpu_custom_call" | custom-call | flops 4294967296 | bytes 14680064 | tf_op jit(solution)/shard_map/pallas_call | solution.py:377
  169.7 30.2 %all-gather.15.cloned.1.call-done.win_ref = bf16[1024,4096]{1,0:T(8,128)(2,1)} async-done(((bf16[128,4096]{1,0:T(8,128)(2,1)}), bf16[1024,4096]{1,0:T(8,128)(2,1)}) %all-gather.15.cloned.1.call-update) | async-done | bytes 8388624 | tf_op jit(solution)/shard_map/all_gather | solution.py:586
  199.9 51.5 %all-gather.17.cloned.1.call-done.wff_ref = bf16[4096,1024]{1,0:T(8,128)(2,1)} async-done(((bf16[512,1024]{1,0:T(8,128)(2,1)}), bf16[4096,1024]{1,0:T(8,128)(2,1)}) %all-gather.17.cloned.1.call-update) | async-done | bytes 8388624 | tf_op jit(solution)/shard_map/all_gather | solution.py:586
  251.4 39.3 %shard_map.297 = (bf16[512,1024]{1,0:T(8,128)(2,1)}, f32[512,1024]{1,0:T(8,128)}, bf16[1024,512]{1,0:T(8,128)(2,1)}, f32[1,512]{1,0:T(1,128)}, bf16[1024,512]{1,0:T(8,128)(2,1)}, /*index=5*/f32[1,1024]{1,0:T(1,128)}) custom-call(s32[2]{0:T(128)} %len_ref.5, f32[512,1024]{1,0:T(8,128)} %get-tuple-element.32.nrm2_ref, f32[512,1]{1,0:T(8,128)} %get-tuple-element.33.inv2_ref, ...), custom_call_target="tpu_custom_call" | custom-call | flops 20401094656 | bytes 33554432 | tf_op jit(solution)/shard_map/pallas_call | solution.py:377
  290.6 25.8 %shard_map.298 = (bf16[512,1024]{1,0:T(8,128)(2,1)}, bf16[768,1024]{1,0:T(8,128)(2,1)}) custom-call(s32[2]{0:T(128)} %dynamic_slice.3.len_ref, f32[512,1024]{1,0:T(8,128)} %get-tuple-element.35.gtwo_ref, bf16[1024,1024]{1,0:T(8,128)(2,1)} %all-gather.13.cloned.1.call-done.wco_ref, bf16[512,1024]{1,0:T(8,128)(2,1)} %get-tuple-element.30.cq_ref, ...), custom_call_target="tpu_custom_call" | custom-call | flops 4294967296 | bytes 14680064 | tf_op jit(solution)/shard_map/pallas_call | solution.py:377
  316.4 31.3 %shard_map.299 = (bf16[512,1024]{1,0:T(8,128)(2,1)}, f32[32,1024]{1,0:T(8,128)}, f32[32,1024]{1,0:T(8,128)}) custom-call(s32[2]{0:T(128)} %len_ref.5, f32[512,1024]{1,0:T(8,128)} %get-tuple-element.35.gtwo_ref, bf16[512,1024]{1,0:T(8,128)(2,1)} %get-tuple-element.38.cdq_ref, bf16[1024,1024]{1,0:T(8,128)(2,1)} %get-tuple-element.69.wcq_ref, ...), custom_call_target="tpu_custom_call" | custom-call | flops 5368709120 | bytes 20971520 | tf_op jit(solution)/shard_map/pallas_call | solution.py:377
  347.8 1.2 copy.48
  349.1 0.2 copy.49
  349.3 1.1 copy.50
  350.4 0.2 copy.51
  350.7 0.5 broadcast.10
  351.2 0.7 reduce.7
  351.9 0.1 reshape_transpose_reshape.7
  352.0 0.7 reduce.8
  352.7 0.1 reshape_transpose_reshape.6
  352.8 0.1 copy.52
  352.9 0.8 copy.54
  353.7 8.9 %all-to-all-start.2 = ((f32[128,1,492]{2,1,0:T(1,128)}), f32[128,1,492]{2,1,0:T(1,128)S(1)}, u32[]{:S(2)}, u32[]{:S(2)}) async-start(f32[128,1,492]{2,1,0:T(1,128)} %copy.54), calls=%async_computation.2 | async-start | bytes 524288 | tf_op jit(solution)/shard_map/all_to_all | solution.py:628
  362.6 2.8 copy.46
  365.4 8.1 %all-to-all-done.2 = f32[128,1,492]{2,1,0:T(1,128)S(1)} async-done(((f32[128,1,492]{2,1,0:T(1,128)}), f32[128,1,492]{2,1,0:T(1,128)S(1)}, u32[]{:S(2)}, u32[]{:S(2)}) %all-to-all-start.2) | async-done | bytes 251936 | tf_op jit(solution)/shard_map/all_to_all | solution.py:628
  373.5 3.7 all-to-all-start.1
  377.2 2.9 pad_maximum_fusion
  380.1 22.5 %all-to-all-done.1 = bf16[2,384,1024]{2,0,1:T(2,128)(2,1)S(1)} async-done(((bf16[2,384,1024]{2,0,1:T(2,128)(2,1)}), bf16[2,384,1024]{2,0,1:T(2,128)(2,1)S(1)}, u32[]{:S(2)}, u32[]{:S(2)}) %all-to-all-start.1) | async-done | bytes 1572896 | tf_op jit(solution)/shard_map/all_to_all | solution.py:617
  402.7 1.1 copy-done
  403.8 4.6 %all-to-all-start.3 = ((bf16[128,16,512]{2,1,0:T(8,128)(2,1)}), bf16[128,16,512]{2,1,0:T(8,128)(2,1)S(1)}, u32[]{:S(2)}, u32[]{:S(2)}) async-start(bf16[128,16,512]{2,1,0:T(8,128)(2,1)} %pad_maximum_fusion), calls=%async_computation.3 | async-start | bytes 4194304 | tf_op jit(solution)/shard_map/all_to_all | solution.py:628
  408.5 0.2 reduce_sum.18
  408.7 0.6 slice.37
  409.3 0.6 slice.39
  409.9 0.1 fusion.1
  409.9 0.1 reshape.73
  410.0 0.7 copy.55
  410.7 0.1 reshape.74
  410.8 0.7 copy.56
  411.5 3.0 copy.47
  414.5 23.7 %all-to-all-done.3 = bf16[128,16,512]{2,1,0:T(8,128)(2,1)S(1)} async-done(((bf16[128,16,512]{2,1,0:T(8,128)(2,1)}), bf16[128,16,512]{2,1,0:T(8,128)(2,1)S(1)}, u32[]{:S(2)}, u32[]{:S(2)}) %all-to-all-start.3) | async-done | bytes 2097184 | tf_op jit(solution)/shard_map/all_to_all | solution.py:628
  438.2 0.4 convert_reduce_fusion
  438.5 0.6 slice_bitcast_fusion
  (36 shorter events, 0.2 us)
Async XLA Ops:
  7.2 39.2 %all-gather.11.cloned.1.call-start = ((), (), s32[]{:S(2)}) async-start(), calls=%async_computation.6 | async-start | bytes 4718592 | tf_op jit(solution)/shard_map/all_gather | solution.py:586
  9.1 78.3 %all-gather.9.cloned.1.call-start = ((), (), s32[]{:S(2)}) async-start(), calls=%async_computation.5 | async-start | bytes 7077888 | tf_op jit(solution)/shard_map/all_gather | solution.py:586
  9.9 105.3 %all-gather.13.cloned.1.call-start = ((), (), s32[]{:S(2)}) async-start(), calls=%async_computation.7 | async-start | bytes 2359296 | tf_op jit(solution)/shard_map/all_gather | solution.py:586
  10.6 138.0 %all-gather.7.cloned.1.call-start = ((), (), s32[]{:S(2)}) async-start(), calls=%async_computation.4 | async-start | bytes 4718592 | tf_op jit(solution)/shard_map/all_gather | solution.py:586
  11.2 188.7 %all-gather.15.cloned.1.call-start = ((), (), s32[]{:S(2)}) async-start(), calls=%async_computation.8 | async-start | bytes 9437184 | tf_op jit(solution)/shard_map/all_gather | solution.py:586
  11.8 8.9 %copy-start.5 = (bf16[128]{0:T(256)(128)(2,1)S(1)}, bf16[128]{0:T(256)(128)(2,1)}, u32[]{:S(2)}) copy-start(bf16[128]{0:T(256)(128)(2,1)} %param.41) | copy-start | bytes 772
  11.8 8.9 %copy-start.10 = (bf16[128]{0:T(256)(128)(2,1)S(1)}, bf16[128]{0:T(256)(128)(2,1)}, u32[]{:S(2)}) copy-start(bf16[128]{0:T(256)(128)(2,1)} %param.36) | copy-start | bytes 772
  11.8 8.9 %copy-start.11 = (bf16[128]{0:T(256)(128)(2,1)S(1)}, bf16[128]{0:T(256)(128)(2,1)}, u32[]{:S(2)}) copy-start(bf16[128]{0:T(256)(128)(2,1)} %param.37) | copy-start | bytes 772
  11.8 8.9 %copy-start.12 = (bf16[128]{0:T(256)(128)(2,1)S(1)}, bf16[128]{0:T(256)(128)(2,1)}, u32[]{:S(2)}) copy-start(bf16[128]{0:T(256)(128)(2,1)} %param.38) | copy-start | bytes 772
  11.8 8.9 %copy-start.13 = (bf16[128]{0:T(256)(128)(2,1)S(1)}, bf16[128]{0:T(256)(128)(2,1)}, u32[]{:S(2)}) copy-start(bf16[128]{0:T(256)(128)(2,1)} %param.39) | copy-start | bytes 772
  11.8 8.9 %copy-start.14 = (bf16[128]{0:T(256)(128)(2,1)S(1)}, bf16[128]{0:T(256)(128)(2,1)}, u32[]{:S(2)}) copy-start(bf16[128]{0:T(256)(128)(2,1)} %param.40) | copy-start | bytes 772
  11.8 21.4 %copy-start.3 = (bf16[30,1024]{1,0:T(8,128)(2,1)S(1)}, bf16[30,1024]{1,0:T(8,128)(2,1)}, u32[]{:S(2)}) copy-start(bf16[30,1024]{1,0:T(8,128)(2,1)} %param.42) | copy-start | bytes 184324
  11.8 22.1 %copy-start.4 = (bf16[30,1024]{1,0:T(8,128)(2,1)S(1)}, bf16[30,1024]{1,0:T(8,128)(2,1)}, u32[]{:S(2)}) copy-start(bf16[30,1024]{1,0:T(8,128)(2,1)} %param.43) | copy-start | bytes 184324
  11.9 22.7 %copy-start.7 = (bf16[1024]{0:T(1024)(128)(2,1)S(1)}, bf16[1024]{0:T(1024)(128)(2,1)}, u32[]{:S(2)}) copy-start(bf16[1024]{0:T(1024)(128)(2,1)} %param.47) | copy-start | bytes 6148
  11.9 23.3 %copy-start.9 = (bf16[512]{0:T(512)(128)(2,1)S(1)}, bf16[512]{0:T(512)(128)(2,1)}, u32[]{:S(2)}) copy-start(bf16[512]{0:T(512)(128)(2,1)} %param.45) | copy-start | bytes 3076
  11.9 23.9 %copy-start.15 = (s32[32]{0:T(128)S(1)}, s32[32]{0:T(128)}, u32[]{:S(2)}) copy-start(s32[32]{0:T(128)} %param.28) | copy-start | bytes 388
  11.9 239.5 %all-gather.17.cloned.1.call-start = ((), (), s32[]{:S(2)}) async-start(), calls=%async_computation.9 | async-start | bytes 9437184 | tf_op jit(solution)/shard_map/all_gather | solution.py:586
  12.5 32.6 %all-to-all-start = ((bf16[32,24,1024]{2,1,0:T(8,128)(2,1)}), bf16[32,24,1024]{2,1,0:T(8,128)(2,1)S(1)}, u32[]{:S(2)}, u32[]{:S(2)}) async-start(bf16[32,24,1024]{2,1,0:T(8,128)(2,1)} %param.25), calls=%async_computation | async-start | bytes 3145728 | tf_op jit(solution)/shard_map/all_to_all | solution.py:601
  347.8 3.4 copy-start.6
  347.8 4.2 copy-start.8
  347.8 14.8 %copy-start.1 = (bf16[768,1024]{1,0:T(8,128)(2,1)S(1)}, bf16[768,1024]{1,0:T(8,128)(2,1)}, u32[]{:S(2)}) copy-start(bf16[768,1024]{1,0:T(8,128)(2,1)} %get-tuple-element.44) | copy-start | bytes 4718596
  353.7 19.8 %all-to-all-start.2 = ((f32[128,1,492]{2,1,0:T(1,128)}), f32[128,1,492]{2,1,0:T(1,128)S(1)}, u32[]{:S(2)}, u32[]{:S(2)}) async-start(f32[128,1,492]{2,1,0:T(1,128)} %copy.54), calls=%async_computation.2 | async-start | bytes 524288 | tf_op jit(solution)/shard_map/all_to_all | solution.py:628
  365.4 11.8 %copy-start.2 = (bf16[1024,512]{1,0:T(8,128)(2,1)S(1)}, bf16[1024,512]{1,0:T(8,128)(2,1)}, u32[]{:S(2)}) copy-start(bf16[1024,512]{1,0:T(8,128)(2,1)} %get-tuple-element.49) | copy-start | bytes 3145732
  373.5 29.1 %all-to-all-start.1 = ((bf16[2,384,1024]{2,0,1:T(2,128)(2,1)}), bf16[2,384,1024]{2,0,1:T(2,128)(2,1)S(1)}, u32[]{:S(2)}, u32[]{:S(2)}) async-start(bf16[2,384,1024]{2,0,1:T(2,128)(2,1)} %copy.46), calls=%async_computation.1 | async-start | bytes 3145728 | tf_op jit(solution)/shard_map/all_to_all | solution.py:617
  402.6 1.1 copy-start
  403.8 34.4 %all-to-all-start.3 = ((bf16[128,16,512]{2,1,0:T(8,128)(2,1)}), bf16[128,16,512]{2,1,0:T(8,128)(2,1)S(1)}, u32[]{:S(2)}, u32[]{:S(2)}) async-start(bf16[128,16,512]{2,1,0:T(8,128)(2,1)} %pad_maximum_fusion), calls=%async_computation.3 | async-start | bytes 4194304 | tf_op jit(solution)/shard_map/all_to_all | solution.py:628
Sparse Core Ops, SparseCore 0:
  10.3 34.6 all-gather.10
  46.7 40.7 all-gather.8
  89.2 25.2 all-gather.12
  116.0 32.5 all-gather.6
  150.2 49.6 all-gather.14
  201.4 49.8 all-gather.16
